TPU v7x, 32 devices: a whole 2x2x4 slice. The times are simulated.
32 devices in a mesh: grp: 2 (over x), blk: 16 (over z, y, core).
Axes of the slice: x: 2, y: 2, z: 4, core: 2. Of those that a mesh axis runs over, the one named last changes fastest.
Arguments:
- embed: bfloat16 [1024, 256], P(('grp', 'blk')), parts along dimension 0, may hold values from -6 to 6
- pair_weight: bfloat16 [256, 64], replicated, may hold values from -0.375 to 0.375
- conv_kernel: bfloat16 [64, 9, 64], replicated, may hold values from -0.25 to 0.25
- dilations: int32 [4], replicated, may hold values from 0 to 3, each once
- tile_order: int32 [32, 2], P(('grp', 'blk')), parts along dimension 0, may hold values from 0 to 1, each once within a row
- cotangent: bfloat16 [32, 2, 64, 1024], P(('grp', 'blk')), parts along dimension 0, may hold values from -6 to 6
Outputs:
- pair_out: bfloat16 [32, 2, 64, 1024], P(('grp', 'blk')), parts along dimension 0
- grad_embed: float32 [1024, 256], P(('grp', 'blk')), parts along dimension 0
- grad_weight: float32 [512, 64], P('grp'), parts along dimension 0
- grad_kernel: float32 [128, 9, 64], P('grp'), parts along dimension 0
There are 2 independent parts, one for each index of `grp`. A program takes and returns all parts, laid end to end along the dimension named above; an argument that names none is the same for every part. Nothing has to cross between parts.
Inputs may be any that keep to these rules, and one draw needn't show every extreme that they name: A permutation of 0 to 3: channel group g uses dilation 2 ** dilations[g]. Each row is a permutation of 0 and 1: slot t of block b holds the tile at diagonal offset tile_order[b, t].
All inputs are finite; a program needn't handle non-finite values.
Results may differ from a plain program's by a relative error of at most 0.003.
The roundings to bfloat16 on the way count: a program that leaves them out, or rounds other values in their place, can miss the bound.
Values may be sent and summed in bfloat16 or wider, within the bound.
No kernel may reach another device: no remote copies, remote signals or barrier semaphores. Data moves between devices by JAX's collectives and lax.ppermute only.
A program may use at most 128 MiB of HBM per device.

v0:
```python
import jax
import jax.numpy as jnp
from jax import lax
from jax.experimental import pallas as pl
from jax.experimental.pallas import tpu as pltpu
from jax.sharding import PartitionSpec as P

GROUPS = 4
HALO = 8
TILE = 32
LANES = 128
TAPS = 9
F32 = jnp.float32
BF16 = jnp.bfloat16
NN = (((1,), (0,)), ((), ()))
NT = (((1,), (1,)), ((), ()))
TN = (((0,), (0,)), ((), ()))


def dot(a, b, dims=NN):
    return lax.dot_general(a, b, dims, preferred_element_type=F32)


def turn(x, by):
    by = by % LANES
    return x if by == 0 else pltpu.roll(x, by, 1)


def lane_ids(rows):
    return lax.broadcasted_iota(jnp.int32, (rows, LANES), 1)


def within(lane, low, high):
    return jnp.logical_and(lane >= low, lane < high)


def one_hot(target, chunks):
    lane = lane_ids(target.shape[0])
    hits = [jnp.where(target == lane + LANES * c, 1.0, 0.0).astype(BF16) for c in range(chunks)]
    return jnp.concatenate(hits, 1)


def row_ids(rows):
    return lax.broadcasted_iota(jnp.int32, (rows, LANES), 0)


def spread_table(chunks):
    x = row_ids(LANES * chunks)
    return one_hot((((x >> 5) & 3) << 7) + ((x >> 7) << 5) + (x & 31), 4)


def swap_table():
    x = row_ids(HALO * TILE)
    return one_hot(((x & 31) << 3) + (x >> 5), 2)


def edge_table():
    x = row_ids(LANES)
    return one_hot(jnp.where((x & 31) < HALO, ((x & 31) << 5) + (x >> 5), -1), 2)


def corner_table(first):
    x = row_ids(HALO * TILE)
    c = (x & 31) - first
    return one_hot(jnp.where(within(c, 0, HALO), ((x >> 5) << 3) + c, -1), 1)


def as_float(flag):
    return jnp.where(flag, 1.0, 0.0).astype(F32)


def place():
    index = lax.axis_index("blk")
    last = lax.axis_size("blk") - 1
    return index, as_float(index % 2 == 0), as_float(index > 0), as_float(index < last)


def corner_shift(flat, spacing):
    width = flat.shape[0] // GROUPS
    lane = lane_ids(width)
    pieces = []
    for g in range(GROUPS):
        d = spacing[g]
        kept = jnp.logical_and(jnp.logical_and(lane < 8 * HALO, (lane >> 3) < d), (lane & 7) < d)
        x = jnp.where(kept, flat[width * g : width * (g + 1)], 0.0)
        pieces.append(pltpu.roll(x, (HALO + 1) * (HALO - d), 1))
    return jnp.concatenate(pieces, 0).astype(BF16)


def tiles_of(order_ref, cot_ref):
    slot = order_ref[0, 0]
    _, _, _, keep = place()
    return cot_ref[slot], (cot_ref[1 - slot].astype(F32) * keep).astype(BF16)


def fetch(sources, targets, sems):
    copies = [
        pltpu.make_async_copy(source, target, sems.at[i])
        for i, (source, target) in enumerate(zip(sources, targets))
    ]
    for copy in copies:
        copy.start()
    return copies


def pack(
    order_hbm, cot_hbm, embed_hbm,
    chip_ref, core_ref,
    order_ref, cot_ref, embed_ref, sems,
):
    copies = fetch((order_hbm, cot_hbm, embed_hbm), (order_ref, cot_ref, embed_ref), sems)
    edge, head, tail = edge_table(), corner_table(0), corner_table(TILE - HALO)
    for copy in copies:
        copy.wait()
    zero, one = tiles_of(order_ref, cot_ref)
    _, even, _, _ = place()
    channels = zero.shape[0]
    moved = dot(
        jnp.concatenate([zero[:, LANES * j : LANES * (j + 1)] for j in range(8)], 0), edge
    )
    columns = []
    for h in range(2):
        total = None
        for j in range(8):
            piece = moved[channels * j : channels * (j + 1), LANES * h : LANES * (h + 1)]
            piece = turn(piece, 4 * j)
            total = piece if total is None else total + piece
        columns.append(total)
    rim = HALO * TILE
    tail_at = TILE * (TILE - HALO)
    up = [zero[:, :rim].astype(F32)] + columns + [dot(one[:, :rim], head)]
    down = [one[:, tail_at:].astype(F32)] + [jnp.zeros_like(x) for x in columns]
    down += [dot(zero[:, tail_at:], tail)]
    up, down = jnp.concatenate(up, 1), jnp.concatenate(down, 1)
    width = up.shape[1]
    both = jnp.concatenate([embed_ref[:, :LANES], embed_ref[:, LANES:]], 0)
    core_ref[:, :width] = (down * even + up * (1.0 - even)).astype(BF16)
    core_ref[:, width:] = both
    chip_ref[:, :width] = (up * even + down * (1.0 - even)).astype(BF16)
    chip_ref[:, width:] = both


RIM_SIDE, RIM_CORNER, RIM_EMBED, RIM = 256, 512, 640, 768


def from_above(core_ref, chip_ref, at):
    _, even, before, _ = place()
    x = chip_ref[:, at].astype(F32) * (even * before)
    return x + core_ref[:, at].astype(F32) * ((1.0 - even) * before)


def from_below(core_ref, chip_ref, at):
    _, even, _, after = place()
    x = core_ref[:, at].astype(F32) * (even * after)
    return x + chip_ref[:, at].astype(F32) * ((1.0 - even) * after)


def prepare(
    order_ref, dil_ref, cot_ref, kern_ref, weight_ref, embed_ref,
    g_ref, dense_ref, tail_ref, flat_ref, both_ref, scaled_ref, spread_ref, meta_ref,
):
    for g in range(GROUPS):
        meta_ref[g] = jnp.left_shift(jnp.int32(1), dil_ref[g])
    meta_ref[GROUPS] = order_ref[0, 0]
    zero, one = tiles_of(order_ref, cot_ref)
    channels = kern_ref.shape[1]
    swap = swap_table()
    tail_at = TILE * (TILE - HALO)
    y_zero = dot(zero[:, tail_at:], swap)
    y_one = dot(one[:, tail_at:], swap)
    lane = lane_ids(channels)
    own_side = within(lane, 72, 80)
    low = lane < 2 * TILE
    pieces = []
    for j in range(4):
        at = slice(LANES * j, LANES * (j + 1))
        later = slice(LANES * (j + 4), LANES * (j + 5))
        pieces.append(
            jnp.concatenate([zero[:, at], one[:, at], zero[:, later], one[:, later]], 1)
        )
    rows = dot(jnp.concatenate(pieces, 0), spread_table(4))
    for j in range(4):
        for m in range(4):
            row = rows[channels * j : channels * (j + 1), LANES * m : LANES * (m + 1)]
            dense_ref[4 * j + m] = row.astype(BF16)
            for h in range(2):
                r = 16 * h + 4 * j + m
                side = turn(y_zero[:, LANES * h : LANES * (h + 1)], 72 - 8 * (r % 16))
                side = jnp.where(own_side, side, 0.0)
                g_ref[r] = jnp.where(low, turn(row, 64 * h), side).astype(BF16)
    for i in range(HALO):
        rest = turn(y_one[:, :LANES], 72 - 8 * i)
        tail_ref[i] = jnp.where(own_side, rest, 0.0).astype(BF16)
    eye = (
        lax.broadcasted_iota(jnp.int32, (channels, channels), 0)
        == lax.broadcasted_iota(jnp.int32, (channels, channels), 1)
    )
    eye = jnp.where(eye, 1.0, 0.0).astype(BF16)
    for u in range(3):
        for v in range(3):
            t = 3 * u + v
            pair = jnp.concatenate([kern_ref[t], kern_ref[3 * v + u]], 0)
            both_ref[channels * t : channels * (t + 1), :] = dot(eye, pair, NT).astype(BF16)
    for t in range(0, TAPS - 1, 2):
        flat_ref[:, channels * t : channels * (t + 2)] = jnp.concatenate(
            [kern_ref[t].astype(F32), kern_ref[t + 1].astype(F32)], 1
        ).astype(BF16)
    flat_ref[:, channels * (TAPS - 1) : channels * TAPS] = kern_ref[TAPS - 1]
    weight = weight_ref[...].astype(F32)
    own = embed_ref[...].astype(F32)
    for r in range(TILE):
        scaled_ref[channels * r : channels * (r + 1), :] = (own[r : r + 1, :] * weight).astype(
            BF16
        )
    inner = jnp.where(lane < 2 * TILE, 1.0, 0.0).astype(BF16)
    beside = jnp.where(own_side, 1.0, 0.0).astype(BF16)

    def spread_rows(i, carry):
        x = jnp.concatenate([g_ref[2 * i], g_ref[2 * i + 1]], 1)
        y = jnp.concatenate([inner, inner], 1), jnp.concatenate([beside, beside], 1)
        y = dot(both_ref[...], jnp.concatenate([x * y[0], x * y[1]], 0))
        spread_ref[2 * i] = y[:, :LANES]
        spread_ref[2 * i + 1] = y[:, LANES:]
        return carry

    lax.fori_loop(0, TILE // 2, spread_rows, 0, unroll=4)


def unpacked(x):
    return jnp.concatenate([x[:TILE], x[TILE:]], 1)


def forward(
    meta_ref, weight_ref, own_ref, chip_ref, core_ref, dense_ref, scaled_ref,
    part_ref, pair_ref, rolled_ref,
    map_ref,
):
    channels = weight_ref.shape[0]
    width = channels // GROUPS
    weight = weight_ref[...].astype(F32)
    own = own_ref[...].astype(F32)
    after = unpacked(from_below(core_ref, chip_ref, slice(RIM_EMBED, RIM)))
    before = unpacked(from_above(core_ref, chip_ref, slice(RIM_EMBED, RIM)))[TILE - HALO :]
    filler = jnp.zeros((LANES - 2 * TILE - HALO, own.shape[1]), F32)
    columns = jnp.concatenate([own, after, filler, before], 0).astype(BF16)
    lane = lane_ids(channels)
    kept = (
        jnp.logical_or(lane < TILE, lane >= LANES - HALO),
        lane < 2 * TILE,
        within(lane, TILE, 2 * TILE),
    )
    for c in range(6):
        part = 0 if c == 0 else (2 if c == 5 else 1)
        if part == 1:
            scaled = scaled_ref[8 * channels * (c - 1) : 8 * channels * c, :]
        else:
            rim = before if part == 0 else after
            scaled = jnp.concatenate(
                [(rim[i : i + 1, :] * weight).astype(BF16) for i in range(HALO)], 0
            )
        pair = dot(scaled, columns, NT).astype(BF16)
        for i in range(8):
            one = pair[channels * i : channels * (i + 1)]
            if part == 1:
                pair_ref[8 * (c - 1) + i] = one
            x = jnp.where(kept[part], jnp.maximum(one.astype(F32), 0.0), 0.0)
            map_ref[8 * c + i] = x.astype(BF16)
    swap = swap_table()

    def gathered(first, per, low, high, move):
        halves = []
        for half in range(2):
            total = None
            for m in range(per):
                piece = map_ref[first + per * half + m].astype(F32)
                piece = jnp.where(within(lane, low, high), piece, 0.0)
                piece = turn(piece, move(m))
                total = piece if total is None else total + piece
            halves.append(total.astype(BF16))
        return jnp.concatenate(halves, 1)

    above = dot(gathered(0, 4, 0, TILE, lambda m: TILE * m), swap)
    below = dot(gathered(8, 16, TILE, TILE + HALO, lambda m: HALO * m - TILE), swap, NT)
    for r in range(TILE):
        half = LANES * (r // 16)
        side = turn(above[:, half : half + LANES], LANES - HALO - HALO * (r % 16))
        map_ref[HALO + r] += jnp.where(lane >= LANES - HALO, side, 0.0).astype(BF16)
    for i in range(HALO):
        half = LANES * (i // 4)
        side = turn(below[:, half : half + LANES], -TILE * (i % 4))
        map_ref[HALO + TILE + i] += jnp.where(lane < TILE, side, 0.0).astype(BF16)

    spacing = [meta_ref[g] for g in range(GROUPS)]
    source = row_ids(LANES)
    to = lane_ids(LANES)
    for g in range(GROUPS):
        tables = []
        for h in range(2):
            half = within(to, 2 * TILE * h, 2 * TILE * (h + 1))
            offset = jnp.where(half, (source - (to - 2 * TILE * h)) & (LANES - 1), LANES)
            hits = [
                jnp.where(offset == (v * spacing[g]) & (LANES - 1), 1.0, 0.0).astype(BF16)
                for v in (-1, 0, 1)
            ]
            tables.append(jnp.concatenate(hits, 1))
        table = jnp.concatenate(tables, 0)
        at = width * g
        for part in range(2):
            low = [map_ref[16 * part + i, at : at + width, :] for i in range(16)]
            high = [map_ref[16 * part + i + 16, at : at + width, :] for i in range(16)]
            x = jnp.concatenate([jnp.concatenate(low, 0), jnp.concatenate(high, 0)], 1)
            y = dot(x, table).astype(BF16)
            for i in range(16):
                for v in range(3):
                    to_row = channels * v + at
                    rolled_ref[16 * part + i, to_row : to_row + width, :] = y[
                        width * i : width * (i + 1), LANES * v : LANES * (v + 1)
                    ]
    part_ref[...] = jnp.zeros_like(part_ref)

    def sum_rows(j, carry):
        stack = jnp.concatenate([taps_of(rolled_ref, spacing, 2 * j + m) for m in range(2)], 1)
        grads = jnp.concatenate([dense_ref[2 * j], dense_ref[2 * j + 1]], 1)
        part_ref[...] += dot(grads, stack, NT)
        return carry

    lax.fori_loop(0, 8, sum_rows, 0, unroll=4)


def taps_of(rolled_ref, spacing, r):
    channels = rolled_ref.shape[1] // 3
    width = channels // GROUPS
    pieces = []
    for u in range(3):
        for v in range(3):
            for g in range(GROUPS):
                at = channels * v + width * g
                pieces.append(rolled_ref[r + HALO + (u - 1) * spacing[g], at : at + width, :])
    return jnp.concatenate(pieces, 0)


def respond(
    meta_ref, flat_ref, rolled_ref, pair_ref, core_ref, chip_ref,
    out_ref,
    rows_ref, share_ref,
):
    channels = flat_ref.shape[0]
    spacing = [meta_ref[g] for g in range(GROUPS)]
    lane = lane_ids(channels)
    low = lane < 2 * TILE
    _, even, _, keep = place()
    corner = core_ref[...] * even + chip_ref[...].astype(F32) * ((1.0 - even) * keep)
    corner = jnp.concatenate([corner, turn(corner, 8 * HALO)], 0)
    share = dot(flat_ref[:, channels * (TAPS - 1) :], corner_shift(corner, spacing))
    share_ref[:HALO] = jnp.zeros((HALO, channels, LANES), F32)
    for i in range(HALO):
        share_ref[HALO + i] = jnp.where(
            lane >= LANES - HALO, turn(share, LANES - HALO - HALO * i), 0.0
        )

    def conv_rows(j, carry):
        for h in range(2):
            r = 4 * j + 2 * h
            stack = jnp.concatenate([taps_of(rolled_ref, spacing, r + m) for m in range(2)], 1)
            response = dot(flat_ref[...], stack)
            for m in range(2):
                row = jnp.where(
                    low,
                    pair_ref[r + m].astype(F32),
                    turn(pair_ref[r + m + 16].astype(F32), 2 * TILE),
                )
                row = row + (response[:, LANES * m : LANES * (m + 1)] + share_ref[r + m])
                at = LANES * (2 * h + m)
                to = pl.ds(pl.multiple_of(channels * j, channels), channels)
                rows_ref[to, at : at + LANES] = row.astype(BF16)
        return carry

    lax.fori_loop(0, 4, conv_rows, 0)
    slot = meta_ref[GROUPS]
    chunks = dot(rows_ref[...], spread_table(4), NT)
    for j in range(4):
        chunk = chunks[channels * j : channels * (j + 1)]
        for h in range(2):
            at = slice(LANES * (j + 4 * h), LANES * (j + 4 * h + 1))
            to = 2 * LANES * h
            out_ref[slot, :, at] = chunk[:, to : to + LANES].astype(BF16)
            out_ref[1 - slot, :, at] = (chunk[:, to + LANES : to + 2 * LANES] * keep).astype(BF16)


def adjoint(
    meta_ref, g_ref, core_ref, chip_ref, tail_ref, both_ref, pair_ref, spread_ref,
    grad_ref,
    above_ref, below_ref,
):
    channels = g_ref.shape[1]
    width = channels // GROUPS
    span = 3 * channels
    lane = lane_ids(channels)
    zeros = jnp.zeros((channels, LANES), BF16)
    above = from_above(core_ref, chip_ref, slice(0, RIM_EMBED))
    below = from_below(core_ref, chip_ref, slice(0, RIM_EMBED))

    def moved(rim, at, to, size, per, i):
        at += LANES * (i // per)
        x = turn(rim[:, at : at + LANES], to - size * (i % per))
        return jnp.where(within(lane, to, to + size), x, 0.0)

    for h in range(HALO // 2):
        upper, lower = [], []
        for i in (2 * h, 2 * h + 1):
            x = moved(above, 0, 0, TILE, 4, i)
            x = x + moved(above, RIM_CORNER, LANES - HALO, HALO, 16, i)
            upper.append(jnp.concatenate([x.astype(BF16), zeros], 0))
            x = moved(below, 0, TILE, TILE, 4, i)
            x = x + moved(below, RIM_CORNER, 2 * TILE, HALO, 16, i)
            y = moved(below, RIM_SIDE, 80, TILE, 4, i).astype(BF16) + tail_ref[i]
            lower.append(jnp.concatenate([x.astype(BF16), y], 0))
        x = dot(both_ref[2 * span :, :], jnp.concatenate(upper, 1))
        y = dot(both_ref[:span, :], jnp.concatenate(lower, 1))
        for m in range(2):
            above_ref[2 * h + m] = x[:, LANES * m : LANES * (m + 1)]
            below_ref[2 * h + m] = y[:, LANES * m : LANES * (m + 1)]
    spacing = [meta_ref[g] for g in range(GROUPS)]
    second = within(lane, TILE, 2 * TILE)

    def gather_row(first, edge):
        def body(i, carry):
            r = first + i
            pieces = []
            for g in range(GROUPS):
                totals = []
                for v in range(3):
                    at = channels * v + width * g
                    tap = slice(at, at + width)
                    total = spread_ref[r, span + at : span + at + width, :]
                    up, down = r - spacing[g], r + spacing[g]
                    if edge < 0:
                        x = spread_ref[jnp.maximum(up, 0), 2 * span + at : 2 * span + at + width, :]
                        y = above_ref[jnp.minimum(up + HALO, HALO - 1), tap, :]
                        total = total + jnp.where(up < 0, y, x)
                    else:
                        total = total + spread_ref[up, 2 * span + at : 2 * span + at + width, :]
                    if edge > 0:
                        x = spread_ref[jnp.minimum(down, TILE - 1), tap, :]
                        y = below_ref[jnp.maximum(down - TILE, 0), tap, :]
                        total = total + jnp.where(down >= TILE, y, x)
                    else:
                        total = total + spread_ref[down, tap, :]
                    totals.append(total)
                pieces.append(
                    totals[1]
                    + pltpu.roll(totals[0], LANES - spacing[g], 1)
                    + pltpu.roll(totals[2], spacing[g], 1)
                )
            grad = jnp.concatenate(pieces, 0)
            grad = grad + jnp.where(second, turn(grad, -48), 0.0)
            own = g_ref[r].astype(F32)
            own = own + jnp.where(pair_ref[r].astype(F32) > 0, grad, 0.0)
            grad_ref[pl.ds(pl.multiple_of(r * channels, channels), channels), :] = jnp.where(
                lane < 2 * TILE, own, 0.0
            ).astype(BF16)
            return carry

        return body

    lax.fori_loop(0, HALO, gather_row(0, -1), 0, unroll=8)
    lax.fori_loop(0, TILE - 2 * HALO, gather_row(HALO, 0), 0, unroll=8)
    lax.fori_loop(0, HALO, gather_row(TILE - HALO, 1), 0, unroll=8)


def project(
    meta_ref, weight_ref, own_ref, core_ref, chip_ref, scaled_ref, grad_ref, part_ref, pair_ref,
    keep_ref, send_ref, side_ref, near_ref,
    sum_ref, kernel_ref,
):
    channels = weight_ref.shape[0]
    weight = weight_ref[...].astype(F32)
    own = own_ref[...].astype(F32)
    columns = jnp.concatenate(
        [own, unpacked(from_below(core_ref, chip_ref, slice(RIM_EMBED, RIM))), jnp.zeros((LANES - 2 * TILE, own.shape[1]), F32)], 0
    ).astype(BF16)
    weight_part = jnp.zeros_like(weight)
    local = []
    for c in range(4):
        at = slice(8 * channels * c, 8 * channels * (c + 1))
        grad_scaled = dot(grad_ref[at, :], columns)
        for i in range(8):
            one = grad_scaled[channels * i : channels * (i + 1)]
            local.append(jnp.sum(one * weight, 0, keepdims=True))
            weight_part = weight_part + one * own[8 * c + i : 8 * c + i + 1, :]
    both = dot(grad_ref[...], scaled_ref[...], TN)
    near_ref[...] = jnp.concatenate(local, 0) + both[:TILE]
    lane = lane_ids(channels)
    rim = from_above(core_ref, chip_ref, slice(0, RIM_SIDE))
    corner, ends = None, None
    for i in range(HALO):
        x = jnp.where(within(lane, TILE, TILE + HALO), pair_ref[i].astype(F32), 0.0)
        x = turn(jnp.maximum(x, 0.0), HALO * i - TILE)
        half = LANES * (i // 4)
        y = turn(rim[:, half : half + LANES], HALO * i - TILE * (i % 4) - (TILE - HALO))
        y = jnp.where(within(lane, HALO * i, HALO * (i + 1)), y, 0.0)
        corner, ends = (x, y) if i == 0 else (corner + x, ends + y)
    spacing = [meta_ref[g] for g in range(GROUPS)]
    share = dot(ends.astype(BF16), corner_shift(corner, spacing), NT)
    last = channels * (TAPS - 1)
    kernel_ref[:, :last] = part_ref[:, :last]
    kernel_ref[:, last:] = part_ref[:, last:] + share
    corner = corner[: channels // 2] + turn(corner[channels // 2 :], 8 * HALO)
    sum_ref[...] = weight_part
    rows = channels // 2
    features = own.shape[1]
    half = lax.axis_index("blk") % 2
    mine = pl.ds(pl.multiple_of(rows * half, rows), rows)
    other = pl.ds(pl.multiple_of(rows * (1 - half), rows), rows)
    keep_ref[:, :features] = sum_ref[mine, :]
    keep_ref[:, features:] = kernel_ref[mine, :]
    side = features + LANES
    for ref in (send_ref, side_ref):
        ref[:, :features] = both[TILE : 2 * TILE].astype(ref.dtype)
        ref[:, features:side] = corner.astype(ref.dtype)
    send_ref[:, side : side + features] = sum_ref[other, :]
    send_ref[:, side + features :] = kernel_ref[other, :]


def finish(
    mine_ref, other_ref, core_ref, chip_ref, near_ref,
    weight_ref, kernel_ref, embed_ref,
):
    index, even, before, _ = place()
    rows = mine_ref.shape[0]
    channels = 2 * rows
    features = weight_ref.shape[1]
    half = index % 2
    for ref, which in ((mine_ref, half), (other_ref, 1 - half)):
        at = pl.ds(pl.multiple_of(rows * which, rows), rows)
        weight_ref[at, :] = ref[:, :features]
        for t in range(TAPS):
            to = features + channels * t
            kernel_ref[t, at, :] = ref[:, to : to + channels]
    carried = core_ref[:, :features] * (1.0 - even) + chip_ref[:, :features].astype(F32) * (even * before)
    embed_ref[...] = near_ref[...] + carried


VMEM = pl.BlockSpec(memory_space=pltpu.VMEM)
SMEM = pl.BlockSpec(memory_space=pltpu.SMEM)
HBM = pl.BlockSpec(memory_space=pltpu.HBM)


def shape(dims, kind):
    return jax.ShapeDtypeStruct(dims, kind)


def call(kernel, outs, scalars, operands, scratch=(), flops=0, moved=0, first=None, room=40):
    specs = [first or SMEM] * scalars + [VMEM] * (len(operands) - scalars)
    return pl.pallas_call(
        kernel,
        out_shape=outs,
        in_specs=specs,
        out_specs=[SMEM if out.dtype == jnp.int32 else VMEM for out in outs],
        scratch_shapes=list(scratch),
        compiler_params=pltpu.CompilerParams(vmem_limit_bytes=room * 1024 * 1024),
        cost_estimate=pl.CostEstimate(flops=flops, bytes_accessed=moved, transcendentals=0),
    )(*operands)


def swap_with(shard, step):
    return lax.ppermute(shard, "blk", [(i, i ^ step) for i in range(lax.axis_size("blk"))])


def swap_stage(shard, even, odd):
    pairs = [(i, i ^ (odd if i % 2 else even)) for i in range(lax.axis_size("blk"))]
    return lax.ppermute(shard, "blk", pairs)


def swap_chips(shard):
    count = lax.axis_size("blk")
    pairs = [(i, (i + (1 if i % 2 else -1)) % count) for i in range(count)]
    return lax.ppermute(shard, "blk", pairs)


def per_device(embed, pair_weight, conv_kernel, dilations, tile_order, cotangent):
    features = embed.shape[1]
    channels = conv_kernel.shape[0]
    count = lax.axis_size("blk")
    weight = pair_weight.T
    taps = jnp.transpose(conv_kernel, (1, 0, 2))
    cot = cotangent.reshape(2, channels, TILE * TILE)
    packed = shape((channels, RIM), BF16)
    body = shape((TILE, channels, LANES), BF16)
    to_chip, to_core = call(
        pack,
        [packed, packed],
        3,
        (tile_order, cot, embed),
        [
            pltpu.SMEM(tile_order.shape, jnp.int32),
            pltpu.VMEM(cot.shape, BF16),
            pltpu.VMEM(embed.shape, BF16),
            pltpu.SemaphoreType.DMA((3,)),
        ],
        flops=10**10,
        moved=10**6,
        first=HBM,
        room=60,
    )
    chip = swap_chips(to_chip)
    core = swap_with(to_core, 1)
    grads, dense, tail, flat, both, scaled, spread, meta = call(
        prepare,
        [
            body,
            shape((TILE // 2, channels, LANES), BF16),
            shape((HALO, channels, LANES), BF16),
            shape((channels, TAPS * channels), BF16),
            shape((TAPS * channels, 2 * channels), BF16),
            shape((TILE * channels, features), BF16),
            shape((TILE, TAPS * channels, LANES), F32),
            shape((2 * GROUPS,), jnp.int32),
        ],
        2,
        (tile_order, dilations, cot, taps, weight, embed),
        flops=2 * 10**8,
        moved=3 * 10**6,
    )
    part, pair, rolled = call(
        forward,
        [
            shape((channels, TAPS * channels), F32),
            body,
            shape((TILE, 3 * channels, LANES), BF16),
        ],
        1,
        (meta, weight, embed, chip, core, dense, scaled),
        [pltpu.VMEM((TILE + 2 * HALO, channels, LANES), BF16)],
        flops=8 * 10**8,
        moved=4 * 10**6,
    )
    (grad_pair,) = call(
        adjoint,
        [shape((TILE * channels, LANES), BF16)],
        1,
        (meta, grads, core, chip, tail, both, pair, spread),
        [pltpu.VMEM((HALO, 3 * channels, LANES), F32)] * 2,
        flops=8 * 10**8,
        moved=4 * 10**6,
    )
    width = features + TAPS * channels
    side = features + LANES
    total, send, sided, near = call(
        project,
        [
            shape((channels // 2, width), F32),
            shape((channels // 2, side + width), F32),
            shape((channels // 2, side), BF16),
            shape((TILE, features), F32),
        ],
        1,
        (meta, weight, embed, core, chip, scaled, grad_pair, part, pair),
        [pltpu.VMEM((channels, features), F32), pltpu.VMEM((channels, TAPS * channels), F32)],
        flops=4 * 10**8,
        moved=4 * 10**6,
    )
    by_core = swap_with(send, 1)
    by_chip = swap_chips(sided)
    total = total + by_core[:, side:]
    by_core = by_core[:, :side]
    steps = [1 << b for b in range(1, count.bit_length() - 1)]
    turns = list(zip(steps[1:] + steps[:1], steps))
    for even, odd in turns[:-1]:
        total = total + swap_stage(total, even, odd)
    rolled, total, by_chip = lax.optimization_barrier((rolled, total, by_chip))
    last = swap_stage(total, *turns[-1])
    (out,) = call(
        respond,
        [shape((2, channels, TILE * TILE), BF16)],
        1,
        (meta, flat, rolled, pair, by_core[:, features:], by_chip[:, features:]),
        [
            pltpu.VMEM((4 * channels, 4 * LANES), BF16),
            pltpu.VMEM((TILE // 2, channels, LANES), F32),
        ],
        flops=2 * 10**8,
        moved=2 * 10**6,
    )
    out, last = lax.optimization_barrier((out, last))
    total = total + last
    rest = swap_with(total, 1)
    grad_weight, grad_kernel, grad_embed = call(
        finish,
        [
            shape((channels, features), F32),
            shape((TAPS, channels, channels), F32),
            shape((TILE, features), F32),
        ],
        0,
        (total, rest, by_core, by_chip, near),
        moved=10**6,
    )
    return (
        out.reshape(1, 2, channels, TILE * TILE),
        grad_embed,
        grad_weight.T,
        jnp.transpose(grad_kernel, (1, 0, 2)),
    )


def solution(mesh):
    placed = (
        P(("grp", "blk"), None),
        P(),
        P(),
        P(),
        P(("grp", "blk"), None),
        P(("grp", "blk"), None, None, None),
    )
    return jax.shard_map(
        per_device,
        mesh=mesh,
        in_specs=placed,
        out_specs=(
            P(("grp", "blk"), None, None, None),
            P(("grp", "blk"), None),
            P("grp", None),
            P("grp", None, None),
        ),
        check_vma=False,
    )
```

profile of v0, /device:TPU:0, one launch (start us, length us, event | category | flops | bytes accessed | tf_op | source)
XLA Modules:
  0.0 38.8 jit_solution(521603457729483514)
XLA Ops:
  0.7 2.1 %shard_map.94 = (bf16[64,768]{1,0:T(8,128)(2,1)}, bf16[64,768]{1,0:T(8,128)(2,1)}) custom-call(s32[1,2]{1,0:T(1,128)} %order_hbm.1, bf16[2,64,1024]{2,1,0:T(8,128)(2,1)} %bitcast.9, bf16[32,256]{1,0:T(8,128)(2,1)} %own_ref.3), custom_call_target="tpu_custom_call" | custom-call | flops 10000000000 | bytes 1000000 | tf_op jit(solution)/shard_map/pallas_call | solution.py:555
  2.8 5.5 %collective-permute-start = (bf16[64,768]{1,0:T(8,128)(2,1)}, bf16[64,768]{1,0:T(8,128)(2,1)S(1)}, u32[]{:S(2)}, u32[]{:S(2)}) collective-permute-start(bf16[64,768]{1,0:T(8,128)(2,1)} %get-tuple-element.31), channel_id=1, source_target_pairs={{0,15},{1,2},{2,1},{3,4},{4,3},{5,6},{6,5},{7,8},{8,7},{9,10},{10,... | collective-permute-start | bytes 294920 | tf_op jit(solution)/shard_map/ppermute | solution.py:578
  8.3 0.0 collective-permute-start.1
  8.3 0.0 copy-done.2
  8.3 3.2 %shard_map.93 = (bf16[32,64,128]{2,1,0:T(8,128)(2,1)S(1)}, bf16[16,64,128]{2,1,0:T(8,128)(2,1)S(1)}, bf16[8,64,128]{2,1,0:T(8,128)(2,1)S(1)}, bf16[64,576]{1,0:T...) custom-call(s32[1,2]{1,0:T(1,128)S(1)} %copy-done.4, ...), custom_call_target="tpu_custom_call" | custom-call | flops 200000000 | bytes 3000000 | tf_op jit(solution)/shard_map/pallas_call | solution.py:555
  11.5 0.0 collective-permute-done.chip_ref
  11.5 0.0 collective-permute-done.1.core_ref
  11.6 3.0 %shard_map.95 = (f32[64,576]{1,0:T(8,128)S(1)}, bf16[32,64,128]{2,1,0:T(8,128)(2,1)S(1)}, bf16[32,192,128]{2,1,0:T(8,128)(2,1)S(1)}) custom-call(s32[8]{0:T(128)S(1)} %get-tuple-element.29.meta_ref, bf16[64,256]{1,0:T(8,128)(2,1)S(1)} %bitcast.7, bf16[32,256]{1,0:T(8,128)(2,1)S(1)} %copy-done.1, bf16[64,768]{1,0:T(8,128)(2,1)S(1)} %collective-permute-done.chip_ref, ...), custom_call_target="tpu_custom_call" | custom-call | flops 800000000 | bytes 4000000 | tf_op jit(solution)/shard_map/pallas_call | solution.py:555
  14.5 2.8 %shard_map.96.grad_ref = bf16[2048,128]{1,0:T(8,128)(2,1)S(1)} custom-call(s32[8]{0:T(128)S(1)} %get-tuple-element.29.meta_ref, bf16[32,64,128]{2,1,0:T(8,128)(2,1)S(1)} %get-tuple-element.36.g_ref, bf16[64,768]{1,0:T(8,128)(2,1)S(1)} %collective-permute-done.1.core_ref, bf16[64,768]{1,0:T(8,128)(2,1)S(1)} %collective-permute-done.chip_ref, ...), custom_call_target="tpu_custom_call" | custom-call | flops 800000000 | bytes 4000000 | tf_op jit(solution)/shard_map/pallas_call | solution.py:555
  17.4 1.2 %shard_map.97 = (f32[32,832]{1,0:T(8,128)S(1)}, f32[32,1216]{1,0:T(8,128)S(1)}, bf16[32,384]{1,0:T(8,128)(2,1)S(1)}, f32[32,256]{1,0:T(8,128)S(1)}) custom-call(s32[8]{0:T(128)S(1)} %get-tuple-element.29.meta_ref, bf16[64,256]{1,0:T(8,128)(2,1)S(1)} %bitcast.8, bf16[32,256]{1,0:T(8,128)(2,1)S(1)} %copy-done.1, ...), custom_call_target="tpu_custom_call" | custom-call | flops 400000000 | bytes 4000000 | tf_op jit(solution)/shard_map/pallas_call | solution.py:555
  18.6 0.6 %collective-permute-start.2 = (f32[32,1216]{1,0:T(8,128)S(1)}, f32[32,1216]{1,0:T(8,128)S(1)}, u32[]{:S(2)}, u32[]{:S(2)}) collective-permute-start(f32[32,1216]{1,0:T(8,128)S(1)} %get-tuple-element.43), channel_id=1, source_target_pairs={{0,1},{1,0},{2,3},{3,2},{4,5},{5,4},{6,7},{7,6},{8,9},{9,8},{10,11... | collective-permute-start | bytes 466952 | tf_op jit(solution)/shard_map/ppermute | solution.py:567
  19.2 1.0 %collective-permute-done.2 = f32[32,1216]{1,0:T(8,128)S(1)} collective-permute-done((f32[32,1216]{1,0:T(8,128)S(1)}, f32[32,1216]{1,0:T(8,128)S(1)}, u32[]{:S(2)}, u32[]{:S(2)}) %collective-permute-start.2) | collective-permute-done | bytes 155680 | tf_op jit(solution)/shard_map/ppermute | solution.py:567
  20.2 0.1 collective-permute-start.3
  20.3 4.8 %collective-permute-done.3 = f32[32,832]{1,0:T(8,128)S(1)} collective-permute-done((f32[32,832]{1,0:T(8,128)S(1)}, f32[32,832]{1,0:T(8,128)S(1)}, u32[]{:S(2)}, u32[]{:S(2)}) %collective-permute-start.3) | collective-permute-done | bytes 106528 | tf_op jit(solution)/shard_map/ppermute | solution.py:572
  25.1 0.5 %collective-permute-start.4 = (f32[32,832]{1,0:T(8,128)S(1)}, f32[32,832]{1,0:T(8,128)S(1)}, u32[]{:S(2)}, u32[]{:S(2)}) collective-permute-start(f32[32,832]{1,0:T(8,128)S(1)} %add.13), channel_id=1, source_target_pairs={{0,8},{1,5},{2,10},{3,7},{4,12},{5,1},{6,14},{7,3},{8,0},{9,13},{1... | collective-permute-start | bytes 319496 | tf_op jit(solution)/shard_map/ppermute | solution.py:572
  25.6 2.3 %collective-permute-start.5 = (bf16[32,384]{1,0:T(8,128)(2,1)S(1)}, bf16[32,384]{1,0:T(8,128)(2,1)S(1)}, u32[]{:S(2)}, u32[]{:S(2)}) collective-permute-start(bf16[32,384]{1,0:T(8,128)(2,1)S(1)} %get-tuple-element.44), channel_id=1, source_target_pairs={{0,15},{1,2},{2,1},{3,4},{4,3},{5,6},{6,5},{7,8},{8,7},{9,10},{10,... | collective-permute-start | bytes 73736 | tf_op jit(solution)/shard_map/ppermute | solution.py:578
  27.9 3.6 %collective-permute-done.4 = f32[32,832]{1,0:T(8,128)S(1)} collective-permute-done((f32[32,832]{1,0:T(8,128)S(1)}, f32[32,832]{1,0:T(8,128)S(1)}, u32[]{:S(2)}, u32[]{:S(2)}) %collective-permute-start.4) | collective-permute-done | bytes 106528 | tf_op jit(solution)/shard_map/ppermute | solution.py:572
  31.5 0.3 collective-permute-done.5.chip_ref
  31.8 0.0 collective-permute-start.6
  31.8 3.0 %shard_map.98 = bf16[2,64,1024]{2,1,0:T(8,128)(2,1)} custom-call(s32[8]{0:T(128)S(1)} %get-tuple-element.29.meta_ref, bf16[64,576]{1,0:T(8,128)(2,1)S(1)} %get-tuple-element.30.flat_ref, bf16[32,192,128]{2,1,0:T(8,128)(2,1)S(1)} %get-tuple-element.45.rolled_ref, bf16[32,64,128]{2,1,0:T(8,128)(2,1)S(1)} %get-tuple-element.39.pair_ref, ...), custom_call_target="tpu_custom_call" | custom-call | flops 200000000 | bytes 2000000 | tf_op jit(solution)/shard_map/pallas_call | solution.py:555
  34.9 1.7 %collective-permute-done.6 = f32[32,832]{1,0:T(8,128)S(1)} collective-permute-done((f32[32,832]{1,0:T(8,128)S(1)}, f32[32,832]{1,0:T(8,128)S(1)}, u32[]{:S(2)}, u32[]{:S(2)}) %collective-permute-start.6) | collective-permute-done | bytes 106528 | tf_op jit(solution)/shard_map/ppermute | solution.py:572
  36.6 0.1 collective-permute-start.7
  36.7 1.3 %collective-permute-done.7.other_ref = f32[32,832]{1,0:T(8,128)S(1)} collective-permute-done((f32[32,832]{1,0:T(8,128)S(1)}, f32[32,832]{1,0:T(8,128)S(1)}, u32[]{:S(2)}, u32[]{:S(2)}) %collective-permute-start.7) | collective-permute-done | bytes 106528 | tf_op jit(solution)/shard_map/ppermute | solution.py:567
  38.0 0.8 %shard_map.99 = (f32[64,256]{1,0:T(8,128)}, f32[9,64,64]{2,1,0:T(8,128)}, f32[32,256]{1,0:T(8,128)}) custom-call(f32[32,832]{1,0:T(8,128)S(1)} %add.15.mine_ref, f32[32,832]{1,0:T(8,128)S(1)} %collective-permute-done.7.other_ref, f32[32,384]{1,0:T(8,128)S(1)} %slice.19.core_ref, bf16[32,384]{1,0:T(8,128)(2,1)S(1)} %collective-permute-done.5.chip_ref, ...), custom_call_target="tpu_custom_call" | custom-call | bytes 1000000 | tf_op jit(solution)/shard_map/pallas_call | solution.py:555
  (18 shorter events, 0.1 us)
Async XLA Ops:
  0.6 7.6 %copy-start = (bf16[256,64]{0,1:T(8,128)(2,1)S(1)}, bf16[256,64]{0,1:T(8,128)(2,1)}, u32[]{:S(2)}) copy-start(bf16[256,64]{0,1:T(8,128)(2,1)} %param.7) | copy-start | bytes 98308
  0.6 7.6 %copy-start.1 = (bf16[32,256]{1,0:T(8,128)(2,1)S(1)}, bf16[32,256]{1,0:T(8,128)(2,1)}, u32[]{:S(2)}) copy-start(bf16[32,256]{1,0:T(8,128)(2,1)} %own_ref.3) | copy-start | bytes 49156
  0.7 7.6 %copy-start.2 = (bf16[1,2,64,1024]{3,2,1,0:T(8,128)(2,1)S(1)}, bf16[1,2,64,1024]{3,2,1,0:T(8,128)(2,1)}, u32[]{:S(2)}) copy-start(bf16[1,2,64,1024]{3,2,1,0:T(8,128)(2,1)} %param.11) | copy-start | bytes 786436
  0.7 7.6 %copy-start.3 = (bf16[64,9,64]{2,0,1:T(8,128)(2,1)S(1)}, bf16[64,9,64]{2,0,1:T(8,128)(2,1)}, u32[]{:S(2)}) copy-start(bf16[64,9,64]{2,0,1:T(8,128)(2,1)} %param.8) | copy-start | bytes 221188
  0.7 7.6 %copy-start.4 = (s32[1,2]{1,0:T(1,128)S(1)}, s32[1,2]{1,0:T(1,128)}, u32[]{:S(2)}) copy-start(s32[1,2]{1,0:T(1,128)} %order_hbm.1) | copy-start | bytes 28
  0.7 7.6 %copy-start.5 = (s32[4]{0:T(128)S(1)}, s32[4]{0:T(128)}, u32[]{:S(2)}) copy-start(s32[4]{0:T(128)} %dil_ref.1) | copy-start | bytes 52
  2.8 8.8 %collective-permute-start = (bf16[64,768]{1,0:T(8,128)(2,1)}, bf16[64,768]{1,0:T(8,128)(2,1)S(1)}, u32[]{:S(2)}, u32[]{:S(2)}) collective-permute-start(bf16[64,768]{1,0:T(8,128)(2,1)} %get-tuple-element.31), channel_id=1, source_target_pairs={{0,15},{1,2},{2,1},{3,4},{4,3},{5,6},{6,5},{7,8},{8,7},{9,10},{10,... | collective-permute-start | bytes 294920 | tf_op jit(solution)/shard_map/ppermute | solution.py:578
  8.3 3.3 %collective-permute-start.1 = (bf16[64,768]{1,0:T(8,128)(2,1)}, bf16[64,768]{1,0:T(8,128)(2,1)S(1)}, u32[]{:S(2)}, u32[]{:S(2)}) collective-permute-start(bf16[64,768]{1,0:T(8,128)(2,1)} %get-tuple-element.32), channel_id=1, source_target_pairs={{0,1},{1,0},{2,3},{3,2},{4,5},{5,4},{6,7},{7,6},{8,9},{9,8},{10,11... | collective-permute-start | bytes 294920 | tf_op jit(solution)/shard_map/ppermute | solution.py:567
  18.6 1.6 %collective-permute-start.2 = (f32[32,1216]{1,0:T(8,128)S(1)}, f32[32,1216]{1,0:T(8,128)S(1)}, u32[]{:S(2)}, u32[]{:S(2)}) collective-permute-start(f32[32,1216]{1,0:T(8,128)S(1)} %get-tuple-element.43), channel_id=1, source_target_pairs={{0,1},{1,0},{2,3},{3,2},{4,5},{5,4},{6,7},{7,6},{8,9},{9,8},{10,11... | collective-permute-start | bytes 466952 | tf_op jit(solution)/shard_map/ppermute | solution.py:567
  20.2 4.9 %collective-permute-start.3 = (f32[32,832]{1,0:T(8,128)S(1)}, f32[32,832]{1,0:T(8,128)S(1)}, u32[]{:S(2)}, u32[]{:S(2)}) collective-permute-start(f32[32,832]{1,0:T(8,128)S(1)} %slice_add_fusion), channel_id=1, source_target_pairs={{0,4},{1,3},{2,6},{3,1},{4,0},{5,7},{6,2},{7,5},{8,12},{9,11},{10,... | collective-permute-start | bytes 319496 | tf_op jit(solution)/shard_map/ppermute | solution.py:572
  25.1 6.4 %collective-permute-start.4 = (f32[32,832]{1,0:T(8,128)S(1)}, f32[32,832]{1,0:T(8,128)S(1)}, u32[]{:S(2)}, u32[]{:S(2)}) collective-permute-start(f32[32,832]{1,0:T(8,128)S(1)} %add.13), channel_id=1, source_target_pairs={{0,8},{1,5},{2,10},{3,7},{4,12},{5,1},{6,14},{7,3},{8,0},{9,13},{1... | collective-permute-start | bytes 319496 | tf_op jit(solution)/shard_map/ppermute | solution.py:572
  25.6 6.2 %collective-permute-start.5 = (bf16[32,384]{1,0:T(8,128)(2,1)S(1)}, bf16[32,384]{1,0:T(8,128)(2,1)S(1)}, u32[]{:S(2)}, u32[]{:S(2)}) collective-permute-start(bf16[32,384]{1,0:T(8,128)(2,1)S(1)} %get-tuple-element.44), channel_id=1, source_target_pairs={{0,15},{1,2},{2,1},{3,4},{4,3},{5,6},{6,5},{7,8},{8,7},{9,10},{10,... | collective-permute-start | bytes 73736 | tf_op jit(solution)/shard_map/ppermute | solution.py:578
  31.8 4.8 %collective-permute-start.6 = (f32[32,832]{1,0:T(8,128)S(1)}, f32[32,832]{1,0:T(8,128)S(1)}, u32[]{:S(2)}, u32[]{:S(2)}) collective-permute-start(f32[32,832]{1,0:T(8,128)S(1)} %add.14), channel_id=1, source_target_pairs={{0,2},{1,9},{2,0},{3,11},{4,6},{5,13},{6,4},{7,15},{8,10},{9,1},{1... | collective-permute-start | bytes 319496 | tf_op jit(solution)/shard_map/ppermute | solution.py:572
  36.6 1.4 %collective-permute-start.7 = (f32[32,832]{1,0:T(8,128)S(1)}, f32[32,832]{1,0:T(8,128)S(1)}, u32[]{:S(2)}, u32[]{:S(2)}) collective-permute-start(f32[32,832]{1,0:T(8,128)S(1)} %add.15.mine_ref), channel_id=1, source_target_pairs={{0,1},{1,0},{2,3},{3,2},{4,5},{5,4},{6,7},{7,6},{8,9},{9,8},{10,11... | collective-permute-start | bytes 319496 | tf_op jit(solution)/shard_map/ppermute | solution.py:567
where the time goes:
time: 39 us; the launch traced here: 38.8 us
  Pallas kernels  16.2 us (42%)
  waiting for transfers between devices  12.7 us (33%)
  starting transfers between devices  9.03 us (23%)
  between operations  0.81 us (2%)
    pallas_call x7, Pallas kernels, call(): pl.pallas_call(kernel, out_shape=outs, in_specs=specs, out_specs=[SMEM if...  16.2 us
    ppermute x3, waiting for transfers between devices, swap_stage(): return lax.ppermute(shard, 'blk', pairs)  10.1 us
    ppermute x2, starting transfers between devices, swap_chips(): return lax.ppermute(shard, 'blk', pairs)  7.84 us
    ppermute x3, waiting for transfers between devices, swap_with(): lax.ppermute(shard, 'blk', [(i, i ^ step) for i in range(lax.axis_size('b...  2.33 us
  transfers between devices with their start and end apart: 8, of which 6 were waited for; matrix products, arithmetic and copies ran while one was open for 0% of the time, Pallas kernels for 16%

commit v1 on v0

--- a/solution.py
+++ b/solution.py
@@ -469,8 +469,8 @@
 
 
 def project(
-    meta_ref, weight_ref, own_ref, core_ref, chip_ref, scaled_ref, grad_ref, part_ref, pair_ref,
-    keep_ref, send_ref, side_ref, near_ref,
+    meta_ref, weight_ref, own_ref, core_ref, chip_ref, grad_ref, part_ref, pair_ref,
+    keep_ref, send_ref, corner_ref, local_ref,
     sum_ref, kernel_ref,
 ):
     channels = weight_ref.shape[0]
@@ -488,8 +488,7 @@
             one = grad_scaled[channels * i : channels * (i + 1)]
             local.append(jnp.sum(one * weight, 0, keepdims=True))
             weight_part = weight_part + one * own[8 * c + i : 8 * c + i + 1, :]
-    both = dot(grad_ref[...], scaled_ref[...], TN)
-    near_ref[...] = jnp.concatenate(local, 0) + both[:TILE]
+    local_ref[...] = jnp.concatenate(local, 0)
     lane = lane_ids(channels)
     rim = from_above(core_ref, chip_ref, slice(0, RIM_SIDE))
     corner, ends = None, None
@@ -514,16 +513,24 @@
     other = pl.ds(pl.multiple_of(rows * (1 - half), rows), rows)
     keep_ref[:, :features] = sum_ref[mine, :]
     keep_ref[:, features:] = kernel_ref[mine, :]
-    side = features + LANES
-    for ref in (send_ref, side_ref):
-        ref[:, :features] = both[TILE : 2 * TILE].astype(ref.dtype)
-        ref[:, features:side] = corner.astype(ref.dtype)
-    send_ref[:, side : side + features] = sum_ref[other, :]
-    send_ref[:, side + features :] = kernel_ref[other, :]
+    corner_ref[...] = corner
+    send_ref[:, :LANES] = corner
+    send_ref[:, LANES : LANES + features] = sum_ref[other, :]
+    send_ref[:, LANES + features :] = kernel_ref[other, :]
+
+
+def embed_terms(grad_ref, scaled_ref, local_ref, corner_ref, near_ref, far_ref, side_ref):
+    both = dot(grad_ref[...], scaled_ref[...], TN)
+    features = both.shape[1]
+    far = both[TILE : 2 * TILE]
+    near_ref[...] = local_ref[...] + both[:TILE]
+    far_ref[...] = far
+    side_ref[:, :features] = far.astype(BF16)
+    side_ref[:, features:] = corner_ref[...].astype(BF16)
 
 
 def finish(
-    mine_ref, other_ref, core_ref, chip_ref, near_ref,
+    mine_ref, other_ref, chip_ref, near_ref,
     weight_ref, kernel_ref, embed_ref,
 ):
     index, even, before, _ = place()
@@ -537,7 +544,8 @@
         for t in range(TAPS):
             to = features + channels * t
             kernel_ref[t, at, :] = ref[:, to : to + channels]
-    carried = core_ref[:, :features] * (1.0 - even) + chip_ref[:, :features].astype(F32) * (even * before)
+    at = features + TAPS * channels
+    carried = other_ref[:, at:] * (1.0 - even) + chip_ref[:, :features].astype(F32) * (even * before)
     embed_ref[...] = near_ref[...] + carried
 
 
@@ -645,27 +653,39 @@
         moved=4 * 10**6,
     )
     width = features + TAPS * channels
-    side = features + LANES
-    total, send, sided, near = call(
+    total, send, corner, local = call(
         project,
         [
             shape((channels // 2, width), F32),
-            shape((channels // 2, side + width), F32),
-            shape((channels // 2, side), BF16),
+            shape((channels // 2, LANES + width), F32),
+            shape((channels // 2, LANES), F32),
             shape((TILE, features), F32),
         ],
         1,
-        (meta, weight, embed, core, chip, scaled, grad_pair, part, pair),
+        (meta, weight, embed, core, chip, grad_pair, part, pair),
         [pltpu.VMEM((channels, features), F32), pltpu.VMEM((channels, TAPS * channels), F32)],
         flops=4 * 10**8,
         moved=4 * 10**6,
     )
     by_core = swap_with(send, 1)
+    near, far, sided = call(
+        embed_terms,
+        [
+            shape((TILE, features), F32),
+            shape((TILE, features), F32),
+            shape((TILE, features + LANES), BF16),
+        ],
+        0,
+        (grad_pair, scaled, local, corner),
+        flops=2 * 10**8,
+        moved=2 * 10**6,
+    )
     by_chip = swap_chips(sided)
-    total = total + by_core[:, side:]
-    by_core = by_core[:, :side]
+    by_core, sided = lax.optimization_barrier((by_core, sided))
+    total = total + by_core[:, LANES:]
+    by_core = by_core[:, :LANES]
     steps = [1 << b for b in range(1, count.bit_length() - 1)]
-    turns = list(zip(steps[1:] + steps[:1], steps))
+    turns = list(zip(steps, steps[1:] + steps[:1]))
     for even, odd in turns[:-1]:
         total = total + swap_stage(total, even, odd)
     rolled, total, by_chip = lax.optimization_barrier((rolled, total, by_chip))
@@ -674,7 +694,7 @@
         respond,
         [shape((2, channels, TILE * TILE), BF16)],
         1,
-        (meta, flat, rolled, pair, by_core[:, features:], by_chip[:, features:]),
+        (meta, flat, rolled, pair, by_core, by_chip[:, features:]),
         [
             pltpu.VMEM((4 * channels, 4 * LANES), BF16),
             pltpu.VMEM((TILE // 2, channels, LANES), F32),
@@ -684,7 +704,7 @@
     )
     out, last = lax.optimization_barrier((out, last))
     total = total + last
-    rest = swap_with(total, 1)
+    rest = swap_with(jnp.concatenate([total, far], 1), 1)
     grad_weight, grad_kernel, grad_embed = call(
         finish,
         [
@@ -693,7 +713,7 @@
             shape((TILE, features), F32),
         ],
         0,
-        (total, rest, by_core, by_chip, near),
+        (total, rest, by_chip, near),
         moved=10**6,
     )
     return (

time: 39 us -> 40.5 us (1.038)
  starting transfers between devices: 9.03 us -> 10.8 us
  waiting for transfers between devices: 12.7 us -> 12.2 us
    ppermute x3, starting transfers between devices: 0.56 us -> 1.99 us  [swap_stage(): return lax.ppermute(shard, 'blk', pairs)]
    ppermute x2, starting transfers between devices: 7.84 us -> 8.24 us  [swap_chips(): return lax.ppermute(shard, 'blk', pairs)]
    pallas_call x7 -> x8, Pallas kernels: 16.2 us -> 16.4 us  [call(): pl.pallas_call(kernel, out_shape=outs, in_specs=specs, out_specs=[SMEM if...]
where the time goes in v1:
time: 40.5 us; the launch traced here: 40.4 us
  Pallas kernels  16.4 us (40%)
  waiting for transfers between devices  12.2 us (30%)
  starting transfers between devices  10.8 us (27%)
  between operations  0.82 us (2%)
    pallas_call x8, Pallas kernels, call(): pl.pallas_call(kernel, out_shape=outs, in_specs=specs, out_specs=[SMEM if...  16.4 us
    ppermute x3, waiting for transfers between devices, swap_stage(): return lax.ppermute(shard, 'blk', pairs)  9.92 us
    ppermute x2, starting transfers between devices, swap_chips(): return lax.ppermute(shard, 'blk', pairs)  8.24 us
    ppermute x3, waiting for transfers between devices, swap_with(): lax.ppermute(shard, 'blk', [(i, i ^ step) for i in range(lax.axis_size('b...  1.99 us
    ppermute x3, starting transfers between devices, swap_stage(): return lax.ppermute(shard, 'blk', pairs)  1.99 us
  transfers between devices with their start and end apart: 8, of which 6 were waited for; matrix products, arithmetic and copies ran while one was open for 0% of the time, Pallas kernels for 16%

profile of v1, /device:TPU:0, one launch (start us, length us, event | category | flops | bytes accessed | tf_op | source)
XLA Modules:
  0.0 40.4 jit_solution(11615491130201251426)
XLA Ops:
  0.7 2.0 %shard_map.94 = (bf16[64,768]{1,0:T(8,128)(2,1)}, bf16[64,768]{1,0:T(8,128)(2,1)}) custom-call(s32[1,2]{1,0:T(1,128)} %order_hbm.1, bf16[2,64,1024]{2,1,0:T(8,128)(2,1)} %bitcast.6, bf16[32,256]{1,0:T(8,128)(2,1)} %own_ref.3), custom_call_target="tpu_custom_call" | custom-call | flops 10000000000 | bytes 1000000 | tf_op jit(solution)/shard_map/pallas_call | solution.py:563
  2.7 5.5 %collective-permute-start = (bf16[64,768]{1,0:T(8,128)(2,1)}, bf16[64,768]{1,0:T(8,128)(2,1)S(1)}, u32[]{:S(2)}, u32[]{:S(2)}) collective-permute-start(bf16[64,768]{1,0:T(8,128)(2,1)} %get-tuple-element.35), channel_id=1, source_target_pairs={{0,15},{1,2},{2,1},{3,4},{4,3},{5,6},{6,5},{7,8},{8,7},{9,10},{10,... | collective-permute-start | bytes 294920 | tf_op jit(solution)/shard_map/ppermute | solution.py:586
  8.3 0.0 collective-permute-start.1
  8.3 3.2 %shard_map.93 = (bf16[32,64,128]{2,1,0:T(8,128)(2,1)S(1)}, bf16[16,64,128]{2,1,0:T(8,128)(2,1)S(1)}, bf16[8,64,128]{2,1,0:T(8,128)(2,1)S(1)}, bf16[64,576]{1,0:T...) custom-call(s32[1,2]{1,0:T(1,128)S(1)} %copy-done.4, ...), custom_call_target="tpu_custom_call" | custom-call | flops 200000000 | bytes 3000000 | tf_op jit(solution)/shard_map/pallas_call | solution.py:563
  11.5 0.0 collective-permute-done.chip_ref
  11.6 3.0 %shard_map.95 = (f32[64,576]{1,0:T(8,128)S(1)}, bf16[32,64,128]{2,1,0:T(8,128)(2,1)S(1)}, bf16[32,192,128]{2,1,0:T(8,128)(2,1)S(1)}) custom-call(s32[8]{0:T(128)S(1)} %get-tuple-element.33.meta_ref, bf16[64,256]{1,0:T(8,128)(2,1)S(1)} %bitcast.10, bf16[32,256]{1,0:T(8,128)(2,1)S(1)} %copy-done.3, bf16[64,768]{1,0:T(8,128)(2,1)S(1)} %collective-permute-done.chip_ref, ...), custom_call_target="tpu_custom_call" | custom-call | flops 800000000 | bytes 4000000 | tf_op jit(solution)/shard_map/pallas_call | solution.py:563
  14.5 2.8 %shard_map.96.grad_ref = bf16[2048,128]{1,0:T(8,128)(2,1)S(1)} custom-call(s32[8]{0:T(128)S(1)} %get-tuple-element.33.meta_ref, bf16[32,64,128]{2,1,0:T(8,128)(2,1)S(1)} %get-tuple-element.40.g_ref, bf16[64,768]{1,0:T(8,128)(2,1)S(1)} %collective-permute-done.1.core_ref, bf16[64,768]{1,0:T(8,128)(2,1)S(1)} %collective-permute-done.chip_ref, ...), custom_call_target="tpu_custom_call" | custom-call | flops 800000000 | bytes 4000000 | tf_op jit(solution)/shard_map/pallas_call | solution.py:563
  17.4 1.1 %shard_map.97 = (f32[32,832]{1,0:T(8,128)S(1)}, f32[32,960]{1,0:T(8,128)S(1)}, f32[32,128]{1,0:T(8,128)S(1)}, f32[32,256]{1,0:T(8,128)S(1)}) custom-call(s32[8]{0:T(128)S(1)} %get-tuple-element.33.meta_ref, bf16[64,256]{1,0:T(8,128)(2,1)S(1)} %bitcast.11, bf16[32,256]{1,0:T(8,128)(2,1)S(1)} %copy-done.3, ...), custom_call_target="tpu_custom_call" | custom-call | flops 400000000 | bytes 4000000 | tf_op jit(solution)/shard_map/pallas_call | solution.py:563
  18.5 0.6 %collective-permute-start.2 = (f32[32,960]{1,0:T(8,128)S(1)}, f32[32,960]{1,0:T(8,128)S(1)}, u32[]{:S(2)}, u32[]{:S(2)}) collective-permute-start(f32[32,960]{1,0:T(8,128)S(1)} %get-tuple-element.47), channel_id=1, source_target_pairs={{0,1},{1,0},{2,3},{3,2},{4,5},{5,4},{6,7},{7,6},{8,9},{9,8},{10,11... | collective-permute-start | bytes 368648 | tf_op jit(solution)/shard_map/ppermute | solution.py:575
  19.0 0.3 shard_map.98
  19.4 0.6 %collective-permute-done.2 = f32[32,960]{1,0:T(8,128)S(1)} collective-permute-done((f32[32,960]{1,0:T(8,128)S(1)}, f32[32,960]{1,0:T(8,128)S(1)}, u32[]{:S(2)}, u32[]{:S(2)}) %collective-permute-start.2) | collective-permute-done | bytes 122912 | tf_op jit(solution)/shard_map/ppermute | solution.py:575
  20.0 0.1 collective-permute-start.3
  20.1 4.8 %collective-permute-done.3 = f32[32,832]{1,0:T(8,128)S(1)} collective-permute-done((f32[32,832]{1,0:T(8,128)S(1)}, f32[32,832]{1,0:T(8,128)S(1)}, u32[]{:S(2)}, u32[]{:S(2)}) %collective-permute-start.3) | collective-permute-done | bytes 106528 | tf_op jit(solution)/shard_map/ppermute | solution.py:580
  24.9 0.1 collective-permute-start.4
  25.0 2.7 %collective-permute-start.5 = (bf16[32,384]{1,0:T(8,128)(2,1)S(1)}, bf16[32,384]{1,0:T(8,128)(2,1)S(1)}, u32[]{:S(2)}, u32[]{:S(2)}) collective-permute-start(bf16[32,384]{1,0:T(8,128)(2,1)S(1)} %get-tuple-element.50), channel_id=1, source_target_pairs={{0,15},{1,2},{2,1},{3,4},{4,3},{5,6},{6,5},{7,8},{8,7},{9,10},{10,... | collective-permute-start | bytes 73736 | tf_op jit(solution)/shard_map/ppermute | solution.py:586
  27.7 3.2 %collective-permute-done.4 = f32[32,832]{1,0:T(8,128)S(1)} collective-permute-done((f32[32,832]{1,0:T(8,128)S(1)}, f32[32,832]{1,0:T(8,128)S(1)}, u32[]{:S(2)}, u32[]{:S(2)}) %collective-permute-start.4) | collective-permute-done | bytes 106528 | tf_op jit(solution)/shard_map/ppermute | solution.py:580
  31.0 0.3 collective-permute-done.5.chip_ref
  31.2 1.8 %collective-permute-start.6 = (f32[32,832]{1,0:T(8,128)S(1)}, f32[32,832]{1,0:T(8,128)S(1)}, u32[]{:S(2)}, u32[]{:S(2)}) collective-permute-start(f32[32,832]{1,0:T(8,128)S(1)} %add.14), channel_id=1, source_target_pairs={{0,8},{1,3},{2,10},{3,1},{4,12},{5,7},{6,14},{7,5},{8,0},{9,11},{1... | collective-permute-start | bytes 319496 | tf_op jit(solution)/shard_map/ppermute | solution.py:580
  33.1 3.0 %shard_map.99 = bf16[2,64,1024]{2,1,0:T(8,128)(2,1)} custom-call(s32[8]{0:T(128)S(1)} %get-tuple-element.33.meta_ref, bf16[64,576]{1,0:T(8,128)(2,1)S(1)} %get-tuple-element.34.flat_ref, bf16[32,192,128]{2,1,0:T(8,128)(2,1)S(1)} %get-tuple-element.52.rolled_ref, bf16[32,64,128]{2,1,0:T(8,128)(2,1)S(1)} %get-tuple-element.43.pair_ref, ...), custom_call_target="tpu_custom_call" | custom-call | flops 200000000 | bytes 2000000 | tf_op jit(solution)/shard_map/pallas_call | solution.py:563
  36.1 1.9 %collective-permute-done.6 = f32[32,832]{1,0:T(8,128)S(1)} collective-permute-done((f32[32,832]{1,0:T(8,128)S(1)}, f32[32,832]{1,0:T(8,128)S(1)}, u32[]{:S(2)}, u32[]{:S(2)}) %collective-permute-start.6) | collective-permute-done | bytes 106528 | tf_op jit(solution)/shard_map/ppermute | solution.py:580
  38.1 0.1 pad_maximum_fusion
  38.1 0.0 collective-permute-start.7
  38.2 1.4 %collective-permute-done.7.other_ref = f32[32,1088]{1,0:T(8,128)S(1)} collective-permute-done((f32[32,1088]{1,0:T(8,128)S(1)}, f32[32,1088]{1,0:T(8,128)S(1)}, u32[]{:S(2)}, u32[]{:S(2)}) %collective-permute-start.7) | collective-permute-done | bytes 139296 | tf_op jit(solution)/shard_map/ppermute | solution.py:575
  39.5 0.9 %shard_map.100 = (f32[64,256]{1,0:T(8,128)}, f32[9,64,64]{2,1,0:T(8,128)}, f32[32,256]{1,0:T(8,128)}) custom-call(f32[32,832]{1,0:T(8,128)S(1)} %add.15.mine_ref, f32[32,1088]{1,0:T(8,128)S(1)} %collective-permute-done.7.other_ref, bf16[32,384]{1,0:T(8,128)(2,1)S(1)} %collective-permute-done.5.chip_ref, f32[32,256]{1,0:T(8,128)S(1)} %get-tuple-element.58.near_ref), custom_call_target="tpu_custom_call" | custom-call | bytes 1000000 | tf_op jit(solution)/shard_map/pallas_call | solution.py:563
  (19 shorter events, 0.1 us)
Async XLA Ops:
  0.6 7.6 %copy-start = (bf16[1,2,64,1024]{3,2,1,0:T(8,128)(2,1)S(1)}, bf16[1,2,64,1024]{3,2,1,0:T(8,128)(2,1)}, u32[]{:S(2)}) copy-start(bf16[1,2,64,1024]{3,2,1,0:T(8,128)(2,1)} %param.11) | copy-start | bytes 786436
  0.6 7.6 %copy-start.1 = (bf16[64,9,64]{2,0,1:T(8,128)(2,1)S(1)}, bf16[64,9,64]{2,0,1:T(8,128)(2,1)}, u32[]{:S(2)}) copy-start(bf16[64,9,64]{2,0,1:T(8,128)(2,1)} %param.8) | copy-start | bytes 221188
  0.7 7.6 %copy-start.2 = (bf16[256,64]{0,1:T(8,128)(2,1)S(1)}, bf16[256,64]{0,1:T(8,128)(2,1)}, u32[]{:S(2)}) copy-start(bf16[256,64]{0,1:T(8,128)(2,1)} %param.7) | copy-start | bytes 98308
  0.7 7.6 %copy-start.3 = (bf16[32,256]{1,0:T(8,128)(2,1)S(1)}, bf16[32,256]{1,0:T(8,128)(2,1)}, u32[]{:S(2)}) copy-start(bf16[32,256]{1,0:T(8,128)(2,1)} %own_ref.3) | copy-start | bytes 49156
  0.7 7.6 %copy-start.4 = (s32[1,2]{1,0:T(1,128)S(1)}, s32[1,2]{1,0:T(1,128)}, u32[]{:S(2)}) copy-start(s32[1,2]{1,0:T(1,128)} %order_hbm.1) | copy-start | bytes 28
  0.7 7.6 %copy-start.5 = (s32[4]{0:T(128)S(1)}, s32[4]{0:T(128)}, u32[]{:S(2)}) copy-start(s32[4]{0:T(128)} %dil_ref.1) | copy-start | bytes 52
  2.7 8.8 %collective-permute-start = (bf16[64,768]{1,0:T(8,128)(2,1)}, bf16[64,768]{1,0:T(8,128)(2,1)S(1)}, u32[]{:S(2)}, u32[]{:S(2)}) collective-permute-start(bf16[64,768]{1,0:T(8,128)(2,1)} %get-tuple-element.35), channel_id=1, source_target_pairs={{0,15},{1,2},{2,1},{3,4},{4,3},{5,6},{6,5},{7,8},{8,7},{9,10},{10,... | collective-permute-start | bytes 294920 | tf_op jit(solution)/shard_map/ppermute | solution.py:586
  8.3 3.3 %collective-permute-start.1 = (bf16[64,768]{1,0:T(8,128)(2,1)}, bf16[64,768]{1,0:T(8,128)(2,1)S(1)}, u32[]{:S(2)}, u32[]{:S(2)}) collective-permute-start(bf16[64,768]{1,0:T(8,128)(2,1)} %get-tuple-element.36), channel_id=1, source_target_pairs={{0,1},{1,0},{2,3},{3,2},{4,5},{5,4},{6,7},{7,6},{8,9},{9,8},{10,11... | collective-permute-start | bytes 294920 | tf_op jit(solution)/shard_map/ppermute | solution.py:575
  18.5 1.5 %collective-permute-start.2 = (f32[32,960]{1,0:T(8,128)S(1)}, f32[32,960]{1,0:T(8,128)S(1)}, u32[]{:S(2)}, u32[]{:S(2)}) collective-permute-start(f32[32,960]{1,0:T(8,128)S(1)} %get-tuple-element.47), channel_id=1, source_target_pairs={{0,1},{1,0},{2,3},{3,2},{4,5},{5,4},{6,7},{7,6},{8,9},{9,8},{10,11... | collective-permute-start | bytes 368648 | tf_op jit(solution)/shard_map/ppermute | solution.py:575
  20.0 4.9 %collective-permute-start.3 = (f32[32,832]{1,0:T(8,128)S(1)}, f32[32,832]{1,0:T(8,128)S(1)}, u32[]{:S(2)}, u32[]{:S(2)}) collective-permute-start(f32[32,832]{1,0:T(8,128)S(1)} %slice_add_fusion), channel_id=1, source_target_pairs={{0,2},{1,5},{2,0},{3,7},{4,6},{5,1},{6,4},{7,3},{8,10},{9,13},{10,... | collective-permute-start | bytes 319496 | tf_op jit(solution)/shard_map/ppermute | solution.py:580
  24.9 6.0 %collective-permute-start.4 = (f32[32,832]{1,0:T(8,128)S(1)}, f32[32,832]{1,0:T(8,128)S(1)}, u32[]{:S(2)}, u32[]{:S(2)}) collective-permute-start(f32[32,832]{1,0:T(8,128)S(1)} %add.13), channel_id=1, source_target_pairs={{0,4},{1,9},{2,6},{3,11},{4,0},{5,13},{6,2},{7,15},{8,12},{9,1},{1... | collective-permute-start | bytes 319496 | tf_op jit(solution)/shard_map/ppermute | solution.py:580
  25.0 6.2 %collective-permute-start.5 = (bf16[32,384]{1,0:T(8,128)(2,1)S(1)}, bf16[32,384]{1,0:T(8,128)(2,1)S(1)}, u32[]{:S(2)}, u32[]{:S(2)}) collective-permute-start(bf16[32,384]{1,0:T(8,128)(2,1)S(1)} %get-tuple-element.50), channel_id=1, source_target_pairs={{0,15},{1,2},{2,1},{3,4},{4,3},{5,6},{6,5},{7,8},{8,7},{9,10},{10,... | collective-permute-start | bytes 73736 | tf_op jit(solution)/shard_map/ppermute | solution.py:586
  31.2 6.8 %collective-permute-start.6 = (f32[32,832]{1,0:T(8,128)S(1)}, f32[32,832]{1,0:T(8,128)S(1)}, u32[]{:S(2)}, u32[]{:S(2)}) collective-permute-start(f32[32,832]{1,0:T(8,128)S(1)} %add.14), channel_id=1, source_target_pairs={{0,8},{1,3},{2,10},{3,1},{4,12},{5,7},{6,14},{7,5},{8,0},{9,11},{1... | collective-permute-start | bytes 319496 | tf_op jit(solution)/shard_map/ppermute | solution.py:580
  38.1 1.4 %collective-permute-start.7 = (f32[32,1088]{1,0:T(8,128)S(1)}, f32[32,1088]{1,0:T(8,128)S(1)}, u32[]{:S(2)}, u32[]{:S(2)}) collective-permute-start(f32[32,1088]{1,0:T(8,128)S(1)} %pad_maximum_fusion), channel_id=1, source_target_pairs={{0,1},{1,0},{2,3},{3,2},{4,5},{5,4},{6,7},{7,6},{8,9},{9,8},{10,11... | collective-permute-start | bytes 417800 | tf_op jit(solution)/shard_map/ppermute | solution.py:575

commit v2 on v1

--- a/solution.py
+++ b/solution.py
@@ -73,6 +73,12 @@
     index = lax.axis_index("blk")
     last = lax.axis_size("blk") - 1
     return index, as_float(index % 2 == 0), as_float(index > 0), as_float(index < last)
+
+
+def half_of(index):
+    for by in (8, 4, 2, 1):
+        index = index ^ (index >> by)
+    return index & 1
 
 
 def corner_shift(flat, spacing):
@@ -508,7 +514,7 @@
     sum_ref[...] = weight_part
     rows = channels // 2
     features = own.shape[1]
-    half = lax.axis_index("blk") % 2
+    half = half_of(lax.axis_index("blk"))
     mine = pl.ds(pl.multiple_of(rows * half, rows), rows)
     other = pl.ds(pl.multiple_of(rows * (1 - half), rows), rows)
     keep_ref[:, :features] = sum_ref[mine, :]
@@ -537,7 +543,7 @@
     rows = mine_ref.shape[0]
     channels = 2 * rows
     features = weight_ref.shape[1]
-    half = index % 2
+    half = half_of(index)
     for ref, which in ((mine_ref, half), (other_ref, 1 - half)):
         at = pl.ds(pl.multiple_of(rows * which, rows), rows)
         weight_ref[at, :] = ref[:, :features]
@@ -575,8 +581,8 @@
     return lax.ppermute(shard, "blk", [(i, i ^ step) for i in range(lax.axis_size("blk"))])
 
 
-def swap_stage(shard, even, odd):
-    pairs = [(i, i ^ (odd if i % 2 else even)) for i in range(lax.axis_size("blk"))]
+def swap_stage(shard, first, second):
+    pairs = [(i, i ^ (second if half_of(i) else first)) for i in range(lax.axis_size("blk"))]
     return lax.ppermute(shard, "blk", pairs)
 
 
@@ -684,10 +690,10 @@
     by_core, sided = lax.optimization_barrier((by_core, sided))
     total = total + by_core[:, LANES:]
     by_core = by_core[:, :LANES]
-    steps = [1 << b for b in range(1, count.bit_length() - 1)]
+    steps = [1 | 1 << b for b in range(1, count.bit_length() - 1)]
     turns = list(zip(steps, steps[1:] + steps[:1]))
-    for even, odd in turns[:-1]:
-        total = total + swap_stage(total, even, odd)
+    for first, second in turns[:-1]:
+        total = total + swap_stage(total, first, second)
     rolled, total, by_chip = lax.optimization_barrier((rolled, total, by_chip))
     last = swap_stage(total, *turns[-1])
     (out,) = call(

time: 40.5 us -> 39.5 us (0.975)
  starting transfers between devices: 10.8 us -> 9.82 us
    ppermute x3, waiting for transfers between devices: 9.92 us -> 7.2 us  [swap_stage(): return lax.ppermute(shard, 'blk', pairs)]
    ppermute x2, waiting for transfers between devices: 0.26 us -> 2.88 us  [swap_chips(): return lax.ppermute(shard, 'blk', pairs)]
    ppermute x3, starting transfers between devices: 1.99 us -> 0.14 us  [swap_stage(): return lax.ppermute(shard, 'blk', pairs)]
    ppermute x2, starting transfers between devices: 8.24 us -> 9.1 us  [swap_chips(): return lax.ppermute(shard, 'blk', pairs)]
  transfers between devices with their start and end apart: 8 -> 8, of which waited for: 6 -> 6; matrix products, arithmetic and copies ran while one was open for 0% -> 0% of each run, Pallas kernels for 16% -> 17%
where the time goes in v2:
time: 39.5 us; the launch traced here: 39.3 us
  Pallas kernels  16.5 us (42%)
  waiting for transfers between devices  12.1 us (31%)
  starting transfers between devices  9.82 us (25%)
  between operations  0.82 us (2%)
    pallas_call x8, Pallas kernels, call(): pl.pallas_call(kernel, out_shape=outs, in_specs=specs, out_specs=[SMEM if...  16.5 us
    ppermute x2, starting transfers between devices, swap_chips(): return lax.ppermute(shard, 'blk', pairs)  9.1 us
    ppermute x3, waiting for transfers between devices, swap_stage(): return lax.ppermute(shard, 'blk', pairs)  7.2 us
    ppermute x2, waiting for transfers between devices, swap_chips(): return lax.ppermute(shard, 'blk', pairs)  2.88 us
    ppermute x3, waiting for transfers between devices, swap_with(): lax.ppermute(shard, 'blk', [(i, i ^ step) for i in range(lax.axis_size('b...  1.99 us
  transfers between devices with their start and end apart: 8, of which 6 were waited for; matrix products, arithmetic and copies ran while one was open for 0% of the time, Pallas kernels for 17%

profile of v2, /device:TPU:0, one launch (start us, length us, event | category | flops | bytes accessed | tf_op | source)
XLA Modules:
  0.0 39.3 jit_solution(9179778894186374444)
XLA Ops:
  0.7 2.0 %shard_map.94 = (bf16[64,768]{1,0:T(8,128)(2,1)}, bf16[64,768]{1,0:T(8,128)(2,1)}) custom-call(s32[1,2]{1,0:T(1,128)} %order_hbm.1, bf16[2,64,1024]{2,1,0:T(8,128)(2,1)} %bitcast.6, bf16[32,256]{1,0:T(8,128)(2,1)} %own_ref.3), custom_call_target="tpu_custom_call" | custom-call | flops 10000000000 | bytes 1000000 | tf_op jit(solution)/shard_map/pallas_call | solution.py:569
  2.7 5.5 %collective-permute-start = (bf16[64,768]{1,0:T(8,128)(2,1)}, bf16[64,768]{1,0:T(8,128)(2,1)S(1)}, u32[]{:S(2)}, u32[]{:S(2)}) collective-permute-start(bf16[64,768]{1,0:T(8,128)(2,1)} %get-tuple-element.35), channel_id=1, source_target_pairs={{0,15},{1,2},{2,1},{3,4},{4,3},{5,6},{6,5},{7,8},{8,7},{9,10},{10,... | collective-permute-start | bytes 294920 | tf_op jit(solution)/shard_map/ppermute | solution.py:592
  8.3 0.0 collective-permute-start.1
  8.3 3.2 %shard_map.93 = (bf16[32,64,128]{2,1,0:T(8,128)(2,1)S(1)}, bf16[16,64,128]{2,1,0:T(8,128)(2,1)S(1)}, bf16[8,64,128]{2,1,0:T(8,128)(2,1)S(1)}, bf16[64,576]{1,0:T...) custom-call(s32[1,2]{1,0:T(1,128)S(1)} %copy-done.4, ...), custom_call_target="tpu_custom_call" | custom-call | flops 200000000 | bytes 3000000 | tf_op jit(solution)/shard_map/pallas_call | solution.py:569
  11.5 0.0 collective-permute-done.chip_ref
  11.6 3.0 %shard_map.95 = (f32[64,576]{1,0:T(8,128)S(1)}, bf16[32,64,128]{2,1,0:T(8,128)(2,1)S(1)}, bf16[32,192,128]{2,1,0:T(8,128)(2,1)S(1)}) custom-call(s32[8]{0:T(128)S(1)} %get-tuple-element.33.meta_ref, bf16[64,256]{1,0:T(8,128)(2,1)S(1)} %bitcast.10, bf16[32,256]{1,0:T(8,128)(2,1)S(1)} %copy-done.3, bf16[64,768]{1,0:T(8,128)(2,1)S(1)} %collective-permute-done.chip_ref, ...), custom_call_target="tpu_custom_call" | custom-call | flops 800000000 | bytes 4000000 | tf_op jit(solution)/shard_map/pallas_call | solution.py:569
  14.5 2.8 %shard_map.96.grad_ref = bf16[2048,128]{1,0:T(8,128)(2,1)S(1)} custom-call(s32[8]{0:T(128)S(1)} %get-tuple-element.33.meta_ref, bf16[32,64,128]{2,1,0:T(8,128)(2,1)S(1)} %get-tuple-element.40.g_ref, bf16[64,768]{1,0:T(8,128)(2,1)S(1)} %collective-permute-done.1.core_ref, bf16[64,768]{1,0:T(8,128)(2,1)S(1)} %collective-permute-done.chip_ref, ...), custom_call_target="tpu_custom_call" | custom-call | flops 800000000 | bytes 4000000 | tf_op jit(solution)/shard_map/pallas_call | solution.py:569
  17.4 1.1 %shard_map.97 = (f32[32,832]{1,0:T(8,128)S(1)}, f32[32,960]{1,0:T(8,128)S(1)}, f32[32,128]{1,0:T(8,128)S(1)}, f32[32,256]{1,0:T(8,128)S(1)}) custom-call(s32[8]{0:T(128)S(1)} %get-tuple-element.33.meta_ref, bf16[64,256]{1,0:T(8,128)(2,1)S(1)} %bitcast.11, bf16[32,256]{1,0:T(8,128)(2,1)S(1)} %copy-done.3, ...), custom_call_target="tpu_custom_call" | custom-call | flops 400000000 | bytes 4000000 | tf_op jit(solution)/shard_map/pallas_call | solution.py:569
  18.5 0.6 %collective-permute-start.2 = (f32[32,960]{1,0:T(8,128)S(1)}, f32[32,960]{1,0:T(8,128)S(1)}, u32[]{:S(2)}, u32[]{:S(2)}) collective-permute-start(f32[32,960]{1,0:T(8,128)S(1)} %get-tuple-element.47), channel_id=1, source_target_pairs={{0,1},{1,0},{2,3},{3,2},{4,5},{5,4},{6,7},{7,6},{8,9},{9,8},{10,11... | collective-permute-start | bytes 368648 | tf_op jit(solution)/shard_map/ppermute | solution.py:581
  19.1 0.3 shard_map.98
  19.4 0.6 %collective-permute-done.2 = f32[32,960]{1,0:T(8,128)S(1)} collective-permute-done((f32[32,960]{1,0:T(8,128)S(1)}, f32[32,960]{1,0:T(8,128)S(1)}, u32[]{:S(2)}, u32[]{:S(2)}) %collective-permute-start.2) | collective-permute-done | bytes 122912 | tf_op jit(solution)/shard_map/ppermute | solution.py:581
  20.1 0.1 collective-permute-start.3
  20.1 4.2 %collective-permute-done.3 = f32[32,832]{1,0:T(8,128)S(1)} collective-permute-done((f32[32,832]{1,0:T(8,128)S(1)}, f32[32,832]{1,0:T(8,128)S(1)}, u32[]{:S(2)}, u32[]{:S(2)}) %collective-permute-start.3) | collective-permute-done | bytes 106528 | tf_op jit(solution)/shard_map/ppermute | solution.py:586
  24.4 0.1 collective-permute-start.4
  24.4 3.6 %collective-permute-start.5 = (bf16[32,384]{1,0:T(8,128)(2,1)S(1)}, bf16[32,384]{1,0:T(8,128)(2,1)S(1)}, u32[]{:S(2)}, u32[]{:S(2)}) collective-permute-start(bf16[32,384]{1,0:T(8,128)(2,1)S(1)} %get-tuple-element.50), channel_id=1, source_target_pairs={{0,15},{1,2},{2,1},{3,4},{4,3},{5,6},{6,5},{7,8},{8,7},{9,10},{10,... | collective-permute-start | bytes 73736 | tf_op jit(solution)/shard_map/ppermute | solution.py:592
  28.0 0.9 %collective-permute-done.4 = f32[32,832]{1,0:T(8,128)S(1)} collective-permute-done((f32[32,832]{1,0:T(8,128)S(1)}, f32[32,832]{1,0:T(8,128)S(1)}, u32[]{:S(2)}, u32[]{:S(2)}) %collective-permute-start.4) | collective-permute-done | bytes 106528 | tf_op jit(solution)/shard_map/ppermute | solution.py:586
  29.0 2.9 %collective-permute-done.5.chip_ref = bf16[32,384]{1,0:T(8,128)(2,1)S(1)} collective-permute-done((bf16[32,384]{1,0:T(8,128)(2,1)S(1)}, bf16[32,384]{1,0:T(8,128)(2,1)S(1)}, u32[]{:S(2)}, u32[]{:S(2)}) %collective-permute-start.5) | collective-permute-done | bytes 24608 | tf_op jit(solution)/shard_map/ppermute | solution.py:592
  31.8 0.0 collective-permute-start.6
  31.9 3.0 %shard_map.99 = bf16[2,64,1024]{2,1,0:T(8,128)(2,1)} custom-call(s32[8]{0:T(128)S(1)} %get-tuple-element.33.meta_ref, bf16[64,576]{1,0:T(8,128)(2,1)S(1)} %get-tuple-element.34.flat_ref, bf16[32,192,128]{2,1,0:T(8,128)(2,1)S(1)} %get-tuple-element.52.rolled_ref, bf16[32,64,128]{2,1,0:T(8,128)(2,1)S(1)} %get-tuple-element.43.pair_ref, ...), custom_call_target="tpu_custom_call" | custom-call | flops 200000000 | bytes 2000000 | tf_op jit(solution)/shard_map/pallas_call | solution.py:569
  34.9 2.1 %collective-permute-done.6 = f32[32,832]{1,0:T(8,128)S(1)} collective-permute-done((f32[32,832]{1,0:T(8,128)S(1)}, f32[32,832]{1,0:T(8,128)S(1)}, u32[]{:S(2)}, u32[]{:S(2)}) %collective-permute-start.6) | collective-permute-done | bytes 106528 | tf_op jit(solution)/shard_map/ppermute | solution.py:586
  37.0 0.1 pad_maximum_fusion
  37.1 0.0 collective-permute-start.7
  37.1 1.4 %collective-permute-done.7.other_ref = f32[32,1088]{1,0:T(8,128)S(1)} collective-permute-done((f32[32,1088]{1,0:T(8,128)S(1)}, f32[32,1088]{1,0:T(8,128)S(1)}, u32[]{:S(2)}, u32[]{:S(2)}) %collective-permute-start.7) | collective-permute-done | bytes 139296 | tf_op jit(solution)/shard_map/ppermute | solution.py:581
  38.4 0.9 %shard_map.100 = (f32[64,256]{1,0:T(8,128)}, f32[9,64,64]{2,1,0:T(8,128)}, f32[32,256]{1,0:T(8,128)}) custom-call(f32[32,832]{1,0:T(8,128)S(1)} %add.15.mine_ref, f32[32,1088]{1,0:T(8,128)S(1)} %collective-permute-done.7.other_ref, bf16[32,384]{1,0:T(8,128)(2,1)S(1)} %collective-permute-done.5.chip_ref, f32[32,256]{1,0:T(8,128)S(1)} %get-tuple-element.58.near_ref), custom_call_target="tpu_custom_call" | custom-call | bytes 1000000 | tf_op jit(solution)/shard_map/pallas_call | solution.py:569
  (19 shorter events, 0.1 us)
Async XLA Ops:
  0.6 7.6 %copy-start = (bf16[1,2,64,1024]{3,2,1,0:T(8,128)(2,1)S(1)}, bf16[1,2,64,1024]{3,2,1,0:T(8,128)(2,1)}, u32[]{:S(2)}) copy-start(bf16[1,2,64,1024]{3,2,1,0:T(8,128)(2,1)} %param.11) | copy-start | bytes 786436
  0.6 7.6 %copy-start.1 = (bf16[64,9,64]{2,0,1:T(8,128)(2,1)S(1)}, bf16[64,9,64]{2,0,1:T(8,128)(2,1)}, u32[]{:S(2)}) copy-start(bf16[64,9,64]{2,0,1:T(8,128)(2,1)} %param.8) | copy-start | bytes 221188
  0.7 7.6 %copy-start.2 = (bf16[256,64]{0,1:T(8,128)(2,1)S(1)}, bf16[256,64]{0,1:T(8,128)(2,1)}, u32[]{:S(2)}) copy-start(bf16[256,64]{0,1:T(8,128)(2,1)} %param.7) | copy-start | bytes 98308
  0.7 7.6 %copy-start.3 = (bf16[32,256]{1,0:T(8,128)(2,1)S(1)}, bf16[32,256]{1,0:T(8,128)(2,1)}, u32[]{:S(2)}) copy-start(bf16[32,256]{1,0:T(8,128)(2,1)} %own_ref.3) | copy-start | bytes 49156
  0.7 7.6 %copy-start.4 = (s32[1,2]{1,0:T(1,128)S(1)}, s32[1,2]{1,0:T(1,128)}, u32[]{:S(2)}) copy-start(s32[1,2]{1,0:T(1,128)} %order_hbm.1) | copy-start | bytes 28
  0.7 7.6 %copy-start.5 = (s32[4]{0:T(128)S(1)}, s32[4]{0:T(128)}, u32[]{:S(2)}) copy-start(s32[4]{0:T(128)} %dil_ref.1) | copy-start | bytes 52
  2.7 8.8 %collective-permute-start = (bf16[64,768]{1,0:T(8,128)(2,1)}, bf16[64,768]{1,0:T(8,128)(2,1)S(1)}, u32[]{:S(2)}, u32[]{:S(2)}) collective-permute-start(bf16[64,768]{1,0:T(8,128)(2,1)} %get-tuple-element.35), channel_id=1, source_target_pairs={{0,15},{1,2},{2,1},{3,4},{4,3},{5,6},{6,5},{7,8},{8,7},{9,10},{10,... | collective-permute-start | bytes 294920 | tf_op jit(solution)/shard_map/ppermute | solution.py:592
  8.3 3.3 %collective-permute-start.1 = (bf16[64,768]{1,0:T(8,128)(2,1)}, bf16[64,768]{1,0:T(8,128)(2,1)S(1)}, u32[]{:S(2)}, u32[]{:S(2)}) collective-permute-start(bf16[64,768]{1,0:T(8,128)(2,1)} %get-tuple-element.36), channel_id=1, source_target_pairs={{0,1},{1,0},{2,3},{3,2},{4,5},{5,4},{6,7},{7,6},{8,9},{9,8},{10,11... | collective-permute-start | bytes 294920 | tf_op jit(solution)/shard_map/ppermute | solution.py:581
  18.5 1.5 %collective-permute-start.2 = (f32[32,960]{1,0:T(8,128)S(1)}, f32[32,960]{1,0:T(8,128)S(1)}, u32[]{:S(2)}, u32[]{:S(2)}) collective-permute-start(f32[32,960]{1,0:T(8,128)S(1)} %get-tuple-element.47), channel_id=1, source_target_pairs={{0,1},{1,0},{2,3},{3,2},{4,5},{5,4},{6,7},{7,6},{8,9},{9,8},{10,11... | collective-permute-start | bytes 368648 | tf_op jit(solution)/shard_map/ppermute | solution.py:581
  20.1 4.3 %collective-permute-start.3 = (f32[32,832]{1,0:T(8,128)S(1)}, f32[32,832]{1,0:T(8,128)S(1)}, u32[]{:S(2)}, u32[]{:S(2)}) collective-permute-start(f32[32,832]{1,0:T(8,128)S(1)} %slice_add_fusion), channel_id=1, source_target_pairs={{0,3},{1,4},{2,7},{3,0},{4,1},{5,6},{6,5},{7,2},{8,13},{9,10},{10,... | collective-permute-start | bytes 319496 | tf_op jit(solution)/shard_map/ppermute | solution.py:586
  24.4 4.6 %collective-permute-start.4 = (f32[32,832]{1,0:T(8,128)S(1)}, f32[32,832]{1,0:T(8,128)S(1)}, u32[]{:S(2)}, u32[]{:S(2)}) collective-permute-start(f32[32,832]{1,0:T(8,128)S(1)} %add.13), channel_id=1, source_target_pairs={{0,5},{1,8},{2,11},{3,6},{4,13},{5,0},{6,3},{7,14},{8,1},{9,12},{1... | collective-permute-start | bytes 319496 | tf_op jit(solution)/shard_map/ppermute | solution.py:586
  24.4 7.4 %collective-permute-start.5 = (bf16[32,384]{1,0:T(8,128)(2,1)S(1)}, bf16[32,384]{1,0:T(8,128)(2,1)S(1)}, u32[]{:S(2)}, u32[]{:S(2)}) collective-permute-start(bf16[32,384]{1,0:T(8,128)(2,1)S(1)} %get-tuple-element.50), channel_id=1, source_target_pairs={{0,15},{1,2},{2,1},{3,4},{4,3},{5,6},{6,5},{7,8},{8,7},{9,10},{10,... | collective-permute-start | bytes 73736 | tf_op jit(solution)/shard_map/ppermute | solution.py:592
  31.8 5.1 %collective-permute-start.6 = (f32[32,832]{1,0:T(8,128)S(1)}, f32[32,832]{1,0:T(8,128)S(1)}, u32[]{:S(2)}, u32[]{:S(2)}) collective-permute-start(f32[32,832]{1,0:T(8,128)S(1)} %add.14), channel_id=1, source_target_pairs={{0,9},{1,2},{2,1},{3,10},{4,7},{5,12},{6,15},{7,4},{8,11},{9,0},{1... | collective-permute-start | bytes 319496 | tf_op jit(solution)/shard_map/ppermute | solution.py:586
  37.1 1.4 %collective-permute-start.7 = (f32[32,1088]{1,0:T(8,128)S(1)}, f32[32,1088]{1,0:T(8,128)S(1)}, u32[]{:S(2)}, u32[]{:S(2)}) collective-permute-start(f32[32,1088]{1,0:T(8,128)S(1)} %pad_maximum_fusion), channel_id=1, source_target_pairs={{0,1},{1,0},{2,3},{3,2},{4,5},{5,4},{6,7},{7,6},{8,9},{9,8},{10,11... | collective-permute-start | bytes 417800 | tf_op jit(solution)/shard_map/ppermute | solution.py:581

commit v3 on v2

--- a/solution.py
+++ b/solution.py
@@ -238,8 +238,7 @@
 
 def forward(
     meta_ref, weight_ref, own_ref, chip_ref, core_ref, dense_ref, scaled_ref,
-    part_ref, pair_ref, rolled_ref,
-    map_ref,
+    part_ref, pair_ref, rolled_ref, map_ref,
 ):
     channels = weight_ref.shape[0]
     width = channels // GROUPS
@@ -356,7 +355,10 @@
     low = lane < 2 * TILE
     _, even, _, keep = place()
     corner = core_ref[...] * even + chip_ref[...].astype(F32) * ((1.0 - even) * keep)
-    corner = jnp.concatenate([corner, turn(corner, 8 * HALO)], 0)
+    low_side, high_side = corner[:, :LANES], corner[:, LANES:]
+    corner = jnp.concatenate(
+        [low_side, turn(low_side, 64), high_side, turn(high_side, 64)], 0
+    )
     share = dot(flat_ref[:, channels * (TAPS - 1) :], corner_shift(corner, spacing))
     share_ref[:HALO] = jnp.zeros((HALO, channels, LANES), F32)
     for i in range(HALO):
@@ -395,8 +397,7 @@
 
 def adjoint(
     meta_ref, g_ref, core_ref, chip_ref, tail_ref, both_ref, pair_ref, spread_ref,
-    grad_ref,
-    above_ref, below_ref,
+    grad_ref, above_ref, below_ref,
 ):
     channels = g_ref.shape[1]
     width = channels // GROUPS
@@ -476,8 +477,7 @@
 
 def project(
     meta_ref, weight_ref, own_ref, core_ref, chip_ref, grad_ref, part_ref, pair_ref,
-    keep_ref, send_ref, corner_ref, local_ref,
-    sum_ref, kernel_ref,
+    keep_ref, send_ref, corner_ref, local_ref, sum_ref, kernel_ref,
 ):
     channels = weight_ref.shape[0]
     weight = weight_ref[...].astype(F32)
@@ -510,29 +510,54 @@
     last = channels * (TAPS - 1)
     kernel_ref[:, :last] = part_ref[:, :last]
     kernel_ref[:, last:] = part_ref[:, last:] + share
-    corner = corner[: channels // 2] + turn(corner[channels // 2 :], 8 * HALO)
+    quarter = channels // 4
+    corner = [corner[quarter * q : quarter * (q + 1)] for q in range(4)]
+    corner = jnp.concatenate(
+        [corner[0] + turn(corner[1], 64), corner[2] + turn(corner[3], 64)], 1
+    )
+    corner_ref[...] = corner
     sum_ref[...] = weight_part
     rows = channels // 2
-    features = own.shape[1]
     half = half_of(lax.axis_index("blk"))
-    mine = pl.ds(pl.multiple_of(rows * half, rows), rows)
-    other = pl.ds(pl.multiple_of(rows * (1 - half), rows), rows)
-    keep_ref[:, :features] = sum_ref[mine, :]
-    keep_ref[:, features:] = kernel_ref[mine, :]
-    corner_ref[...] = corner
-    send_ref[:, :LANES] = corner
-    send_ref[:, LANES : LANES + features] = sum_ref[other, :]
-    send_ref[:, LANES + features :] = kernel_ref[other, :]
+    send_ref[:quarter] = corner
+    for ref, which, first in ((keep_ref, half, 0), (send_ref, 1 - half, quarter)):
+        at = pl.multiple_of(rows * which, rows)
+        ref[first : first + rows] = sum_ref[pl.ds(at, rows), :]
+        for q in range(2):
+            to = first + rows * (q + 1)
+            ref[to : to + rows] = kernel_ref[pl.ds(at, rows), 256 * q : 256 * (q + 1)]
+        ref[first + 3 * rows :] = jnp.concatenate(
+            [kernel_ref[pl.ds(at + 8 * q, 8), 512:] for q in range(4)], 1
+        )
+
+
+def middle(
+    meta_ref, weight_ref, own_ref, chip_ref, core_ref, dense_ref, scaled_ref, g_ref, tail_ref,
+    both_ref, spread_ref,
+    keep_ref, send_ref, corner_ref, local_ref, grad_ref, pair_ref, rolled_ref,
+    map_ref, part_ref, above_ref, below_ref, sum_ref, kernel_ref,
+):
+    forward(
+        meta_ref, weight_ref, own_ref, chip_ref, core_ref, dense_ref, scaled_ref,
+        part_ref, pair_ref, rolled_ref, map_ref,
+    )
+    adjoint(
+        meta_ref, g_ref, core_ref, chip_ref, tail_ref, both_ref, pair_ref, spread_ref,
+        grad_ref, above_ref, below_ref,
+    )
+    project(
+        meta_ref, weight_ref, own_ref, core_ref, chip_ref, grad_ref, part_ref, pair_ref,
+        keep_ref, send_ref, corner_ref, local_ref, sum_ref, kernel_ref,
+    )
 
 
 def embed_terms(grad_ref, scaled_ref, local_ref, corner_ref, near_ref, far_ref, side_ref):
     both = dot(grad_ref[...], scaled_ref[...], TN)
-    features = both.shape[1]
     far = both[TILE : 2 * TILE]
     near_ref[...] = local_ref[...] + both[:TILE]
     far_ref[...] = far
-    side_ref[:, :features] = far.astype(BF16)
-    side_ref[:, features:] = corner_ref[...].astype(BF16)
+    side_ref[:TILE] = far.astype(BF16)
+    side_ref[TILE:] = corner_ref[...].astype(BF16)
 
 
 def finish(
@@ -540,18 +565,22 @@
     weight_ref, kernel_ref, embed_ref,
 ):
     index, even, before, _ = place()
-    rows = mine_ref.shape[0]
-    channels = 2 * rows
-    features = weight_ref.shape[1]
+    channels = kernel_ref.shape[1]
+    rows = channels // 2
     half = half_of(index)
     for ref, which in ((mine_ref, half), (other_ref, 1 - half)):
-        at = pl.ds(pl.multiple_of(rows * which, rows), rows)
-        weight_ref[at, :] = ref[:, :features]
-        for t in range(TAPS):
-            to = features + channels * t
-            kernel_ref[t, at, :] = ref[:, to : to + channels]
-    at = features + TAPS * channels
-    carried = other_ref[:, at:] * (1.0 - even) + chip_ref[:, :features].astype(F32) * (even * before)
+        at = pl.multiple_of(rows * which, rows)
+        weight_ref[pl.ds(at, rows), :] = ref[:rows]
+        for t in range(TAPS - 1):
+            first = rows * (1 + t // 4)
+            to = channels * (t % 4)
+            kernel_ref[t, pl.ds(at, rows), :] = ref[first : first + rows, to : to + channels]
+        for q in range(4):
+            kernel_ref[TAPS - 1, pl.ds(at + 8 * q, 8), :] = ref[
+                3 * rows : 3 * rows + 8, channels * q : channels * (q + 1)
+            ]
+    carried = other_ref[3 * rows + 8 :] * (1.0 - even)
+    carried = carried + chip_ref[...].astype(F32) * (even * before)
     embed_ref[...] = near_ref[...] + carried
 
 
@@ -564,7 +593,7 @@
     return jax.ShapeDtypeStruct(dims, kind)
 
 
-def call(kernel, outs, scalars, operands, scratch=(), flops=0, moved=0, first=None, room=40):
+def call(kernel, outs, scalars, operands, scratch=(), flops=0, moved=0, first=None, room=32):
     specs = [first or SMEM] * scalars + [VMEM] * (len(operands) - scalars)
     return pl.pallas_call(
         kernel,
@@ -636,42 +665,32 @@
         flops=2 * 10**8,
         moved=3 * 10**6,
     )
-    part, pair, rolled = call(
-        forward,
+    rows = channels // 2
+    sums = 3 * rows + rows * channels // features
+    total, send, corner, local, grad_pair, pair, rolled = call(
+        middle,
         [
-            shape((channels, TAPS * channels), F32),
+            shape((sums, features), F32),
+            shape((channels // 4 + sums, features), F32),
+            shape((channels // 4, features), F32),
+            shape((TILE, features), F32),
+            shape((TILE * channels, LANES), BF16),
             body,
             shape((TILE, 3 * channels, LANES), BF16),
         ],
         1,
-        (meta, weight, embed, chip, core, dense, scaled),
-        [pltpu.VMEM((TILE + 2 * HALO, channels, LANES), BF16)],
-        flops=8 * 10**8,
-        moved=4 * 10**6,
-    )
-    (grad_pair,) = call(
-        adjoint,
-        [shape((TILE * channels, LANES), BF16)],
-        1,
-        (meta, grads, core, chip, tail, both, pair, spread),
-        [pltpu.VMEM((HALO, 3 * channels, LANES), F32)] * 2,
-        flops=8 * 10**8,
-        moved=4 * 10**6,
-    )
-    width = features + TAPS * channels
-    total, send, corner, local = call(
-        project,
+        (meta, weight, embed, chip, core, dense, scaled, grads, tail, both, spread),
         [
-            shape((channels // 2, width), F32),
-            shape((channels // 2, LANES + width), F32),
-            shape((channels // 2, LANES), F32),
-            shape((TILE, features), F32),
+            pltpu.VMEM((TILE + 2 * HALO, channels, LANES), BF16),
+            pltpu.VMEM((channels, TAPS * channels), F32),
+            pltpu.VMEM((HALO, 3 * channels, LANES), F32),
+            pltpu.VMEM((HALO, 3 * channels, LANES), F32),
+            pltpu.VMEM((channels, features), F32),
+            pltpu.VMEM((channels, TAPS * channels), F32),
         ],
-        1,
-        (meta, weight, embed, core, chip, grad_pair, part, pair),
-        [pltpu.VMEM((channels, features), F32), pltpu.VMEM((channels, TAPS * channels), F32)],
-        flops=4 * 10**8,
-        moved=4 * 10**6,
+        flops=2 * 10**9,
+        moved=8 * 10**6,
+        room=24,
     )
     by_core = swap_with(send, 1)
     near, far, sided = call(
@@ -679,7 +698,7 @@
         [
             shape((TILE, features), F32),
             shape((TILE, features), F32),
-            shape((TILE, features + LANES), BF16),
+            shape((TILE + channels // 4, features), BF16),
         ],
         0,
         (grad_pair, scaled, local, corner),
@@ -688,8 +707,8 @@
     )
     by_chip = swap_chips(sided)
     by_core, sided = lax.optimization_barrier((by_core, sided))
-    total = total + by_core[:, LANES:]
-    by_core = by_core[:, :LANES]
+    total = total + by_core[channels // 4 :]
+    by_core = by_core[: channels // 4]
     steps = [1 | 1 << b for b in range(1, count.bit_length() - 1)]
     turns = list(zip(steps, steps[1:] + steps[:1]))
     for first, second in turns[:-1]:
@@ -700,7 +719,7 @@
         respond,
         [shape((2, channels, TILE * TILE), BF16)],
         1,
-        (meta, flat, rolled, pair, by_core, by_chip[:, features:]),
+        (meta, flat, rolled, pair, by_core, by_chip[TILE:]),
         [
             pltpu.VMEM((4 * channels, 4 * LANES), BF16),
             pltpu.VMEM((TILE // 2, channels, LANES), F32),
@@ -710,7 +729,7 @@
     )
     out, last = lax.optimization_barrier((out, last))
     total = total + last
-    rest = swap_with(jnp.concatenate([total, far], 1), 1)
+    rest = swap_with(jnp.concatenate([total, far]), 1)
     grad_weight, grad_kernel, grad_embed = call(
         finish,
         [
@@ -719,7 +738,7 @@
             shape((TILE, features), F32),
         ],
         0,
-        (total, rest, by_chip, near),
+        (total, rest, by_chip[:TILE], near),
         moved=10**6,
     )
     return (

time: 39.5 us -> 37.8 us (0.957)
  Pallas kernels: 16.5 us -> 15.2 us
  waiting for transfers between devices: 12.1 us -> 11.7 us
    pallas_call x8 -> x6, Pallas kernels: 16.5 us -> 15.2 us  [call(): pl.pallas_call(kernel, out_shape=outs, in_specs=specs, out_specs=[SMEM if...]
  transfers between devices with their start and end apart: 8 -> 8, of which waited for: 6 -> 6; matrix products, arithmetic and copies ran while one was open for 0% -> 0% of each run, Pallas kernels for 17% -> 18%
where the time goes in v3:
time: 37.8 us; the launch traced here: 37.6 us
  Pallas kernels  15.2 us (40%)
  waiting for transfers between devices  11.7 us (31%)
  starting transfers between devices  9.84 us (26%)
  between operations  0.81 us (2%)
    pallas_call x6, Pallas kernels, call(): pl.pallas_call(kernel, out_shape=outs, in_specs=specs, out_specs=[SMEM if...  15.2 us
    ppermute x2, starting transfers between devices, swap_chips(): return lax.ppermute(shard, 'blk', pairs)  9.08 us
    ppermute x3, waiting for transfers between devices, swap_stage(): return lax.ppermute(shard, 'blk', pairs)  6.91 us
    ppermute x2, waiting for transfers between devices, swap_chips(): return lax.ppermute(shard, 'blk', pairs)  2.82 us
    ppermute x3, waiting for transfers between devices, swap_with(): lax.ppermute(shard, 'blk', [(i, i ^ step) for i in range(lax.axis_size('b...  1.96 us
  transfers between devices with their start and end apart: 8, of which 6 were waited for; matrix products, arithmetic and copies ran while one was open for 0% of the time, Pallas kernels for 18%

profile of v3, /device:TPU:0, one launch (start us, length us, event | category | flops | bytes accessed | tf_op | source)
XLA Modules:
  0.0 37.6 jit_solution(16806234218327212062)
XLA Ops:
  0.6 0.0 copy-start
  0.6 0.0 copy-start.1
  0.7 2.1 %shard_map.94 = (bf16[64,768]{1,0:T(8,128)(2,1)}, bf16[64,768]{1,0:T(8,128)(2,1)}) custom-call(s32[1,2]{1,0:T(1,128)} %order_hbm.1, bf16[2,64,1024]{2,1,0:T(8,128)(2,1)} %bitcast.8, bf16[32,256]{1,0:T(8,128)(2,1)} %own_ref.1), custom_call_target="tpu_custom_call" | custom-call | flops 10000000000 | bytes 1000000 | tf_op jit(solution)/shard_map/pallas_call | solution.py:598
  2.8 5.5 %collective-permute-start = (bf16[64,768]{1,0:T(8,128)(2,1)}, bf16[64,768]{1,0:T(8,128)(2,1)S(1)}, u32[]{:S(2)}, u32[]{:S(2)}) collective-permute-start(bf16[64,768]{1,0:T(8,128)(2,1)} %get-tuple-element.35), channel_id=1, source_target_pairs={{0,15},{1,2},{2,1},{3,4},{4,3},{5,6},{6,5},{7,8},{8,7},{9,10},{10,... | collective-permute-start | bytes 294920 | tf_op jit(solution)/shard_map/ppermute | solution.py:621
  8.3 0.0 collective-permute-start.1
  8.3 3.2 %shard_map.93 = (bf16[32,64,128]{2,1,0:T(8,128)(2,1)S(1)}, bf16[16,64,128]{2,1,0:T(8,128)(2,1)S(1)}, bf16[8,64,128]{2,1,0:T(8,128)(2,1)S(1)}, bf16[64,576]{1,0:T...) custom-call(s32[1,2]{1,0:T(1,128)S(1)} %copy-done.4, ...), custom_call_target="tpu_custom_call" | custom-call | flops 200000000 | bytes 3000000 | tf_op jit(solution)/shard_map/pallas_call | solution.py:598
  11.5 0.0 collective-permute-done.chip_ref
  11.5 0.0 collective-permute-done.1.core_ref
  11.6 5.7 %shard_map.95 = (f32[104,256]{1,0:T(8,128)S(1)}, f32[120,256]{1,0:T(8,128)S(1)}, f32[16,256]{1,0:T(8,128)S(1)}, f32[32,256]{1,0:T(8,128)S(1)}, bf16[2048,128]{1,...) custom-call(s32[8]{0:T(128)S(1)} %get-tuple-element.33.meta_ref, ...), custom_call_target="tpu_custom_call" | custom-call | flops 2000000000 | bytes 8000000 | tf_op jit(solution)/shard_map/pallas_call | solution.py:598
  17.3 0.5 %collective-permute-start.2 = (f32[120,256]{1,0:T(8,128)S(1)}, f32[120,256]{1,0:T(8,128)S(1)}, u32[]{:S(2)}, u32[]{:S(2)}) collective-permute-start(f32[120,256]{1,0:T(8,128)S(1)} %get-tuple-element.45), channel_id=1, source_target_pairs={{0,1},{1,0},{2,3},{3,2},{4,5},{5,4},{6,7},{7,6},{8,9},{9,8},{10,11... | collective-permute-start | bytes 368648 | tf_op jit(solution)/shard_map/ppermute | solution.py:610
  17.8 0.3 shard_map.96
  18.2 0.6 %collective-permute-done.2 = f32[120,256]{1,0:T(8,128)S(1)} collective-permute-done((f32[120,256]{1,0:T(8,128)S(1)}, f32[120,256]{1,0:T(8,128)S(1)}, u32[]{:S(2)}, u32[]{:S(2)}) %collective-permute-start.2) | collective-permute-done | bytes 122912 | tf_op jit(solution)/shard_map/ppermute | solution.py:610
  18.8 0.1 collective-permute-start.3
  18.9 4.1 %collective-permute-done.3 = f32[104,256]{1,0:T(8,128)S(1)} collective-permute-done((f32[104,256]{1,0:T(8,128)S(1)}, f32[104,256]{1,0:T(8,128)S(1)}, u32[]{:S(2)}, u32[]{:S(2)}) %collective-permute-start.3) | collective-permute-done | bytes 106528 | tf_op jit(solution)/shard_map/ppermute | solution.py:615
  23.0 0.1 collective-permute-start.4
  23.1 3.6 %collective-permute-start.5 = (bf16[48,256]{1,0:T(8,128)(2,1)S(1)}, bf16[48,256]{1,0:T(8,128)(2,1)S(1)}, u32[]{:S(2)}, u32[]{:S(2)}) collective-permute-start(bf16[48,256]{1,0:T(8,128)(2,1)S(1)} %get-tuple-element.49), channel_id=1, source_target_pairs={{0,15},{1,2},{2,1},{3,4},{4,3},{5,6},{6,5},{7,8},{8,7},{9,10},{10,... | collective-permute-start | bytes 73736 | tf_op jit(solution)/shard_map/ppermute | solution.py:621
  26.7 0.8 %collective-permute-done.4 = f32[104,256]{1,0:T(8,128)S(1)} collective-permute-done((f32[104,256]{1,0:T(8,128)S(1)}, f32[104,256]{1,0:T(8,128)S(1)}, u32[]{:S(2)}, u32[]{:S(2)}) %collective-permute-start.4) | collective-permute-done | bytes 106528 | tf_op jit(solution)/shard_map/ppermute | solution.py:615
  27.5 2.8 %collective-permute-done.5 = bf16[48,256]{1,0:T(8,128)(2,1)S(1)} collective-permute-done((bf16[48,256]{1,0:T(8,128)(2,1)S(1)}, bf16[48,256]{1,0:T(8,128)(2,1)S(1)}, u32[]{:S(2)}, u32[]{:S(2)}) %collective-permute-start.5) | collective-permute-done | bytes 24608 | tf_op jit(solution)/shard_map/ppermute | solution.py:621
  30.3 0.0 collective-permute-start.6
  30.3 3.0 %shard_map.97 = bf16[2,64,1024]{2,1,0:T(8,128)(2,1)} custom-call(s32[8]{0:T(128)S(1)} %get-tuple-element.33.meta_ref, bf16[64,576]{1,0:T(8,128)(2,1)S(1)} %get-tuple-element.34.flat_ref, bf16[32,192,128]{2,1,0:T(8,128)(2,1)S(1)} %get-tuple-element.51.rolled_ref, bf16[32,64,128]{2,1,0:T(8,128)(2,1)S(1)} %get-tuple-element.52.pair_ref, ...), custom_call_target="tpu_custom_call" | custom-call | flops 200000000 | bytes 2000000 | tf_op jit(solution)/shard_map/pallas_call | solution.py:598
  33.3 2.0 %collective-permute-done.6 = f32[104,256]{1,0:T(8,128)S(1)} collective-permute-done((f32[104,256]{1,0:T(8,128)S(1)}, f32[104,256]{1,0:T(8,128)S(1)}, u32[]{:S(2)}, u32[]{:S(2)}) %collective-permute-start.6) | collective-permute-done | bytes 106528 | tf_op jit(solution)/shard_map/ppermute | solution.py:615
  35.4 0.1 collective-permute-start.7
  35.5 1.3 %collective-permute-done.7.other_ref = f32[136,256]{1,0:T(8,128)S(1)} collective-permute-done((f32[136,256]{1,0:T(8,128)S(1)}, f32[136,256]{1,0:T(8,128)S(1)}, u32[]{:S(2)}, u32[]{:S(2)}) %collective-permute-start.7) | collective-permute-done | bytes 139296 | tf_op jit(solution)/shard_map/ppermute | solution.py:610
  36.8 0.8 %shard_map.98 = (f32[64,256]{1,0:T(8,128)}, f32[9,64,64]{2,1,0:T(8,128)}, f32[32,256]{1,0:T(8,128)}) custom-call(f32[104,256]{1,0:T(8,128)S(1)} %add.15.mine_ref, f32[136,256]{1,0:T(8,128)S(1)} %collective-permute-done.7.other_ref, bf16[32,256]{1,0:T(8,128)(2,1)S(1)} %slice.15.chip_ref, f32[32,256]{1,0:T(8,128)S(1)} %get-tuple-element.58.near_ref), custom_call_target="tpu_custom_call" | custom-call | bytes 1000000 | tf_op jit(solution)/shard_map/pallas_call | solution.py:598
  (18 shorter events, 0.1 us)
Async XLA Ops:
  0.6 7.6 %copy-start = (bf16[256,64]{0,1:T(8,128)(2,1)S(1)}, bf16[256,64]{0,1:T(8,128)(2,1)}, u32[]{:S(2)}) copy-start(bf16[256,64]{0,1:T(8,128)(2,1)} %param.7) | copy-start | bytes 98308
  0.6 7.6 %copy-start.1 = (bf16[32,256]{1,0:T(8,128)(2,1)S(1)}, bf16[32,256]{1,0:T(8,128)(2,1)}, u32[]{:S(2)}) copy-start(bf16[32,256]{1,0:T(8,128)(2,1)} %own_ref.1) | copy-start | bytes 49156
  0.7 7.6 %copy-start.2 = (bf16[1,2,64,1024]{3,2,1,0:T(8,128)(2,1)S(1)}, bf16[1,2,64,1024]{3,2,1,0:T(8,128)(2,1)}, u32[]{:S(2)}) copy-start(bf16[1,2,64,1024]{3,2,1,0:T(8,128)(2,1)} %param.11) | copy-start | bytes 786436
  0.7 7.6 %copy-start.3 = (bf16[64,9,64]{2,0,1:T(8,128)(2,1)S(1)}, bf16[64,9,64]{2,0,1:T(8,128)(2,1)}, u32[]{:S(2)}) copy-start(bf16[64,9,64]{2,0,1:T(8,128)(2,1)} %param.8) | copy-start | bytes 221188
  0.7 7.6 %copy-start.4 = (s32[1,2]{1,0:T(1,128)S(1)}, s32[1,2]{1,0:T(1,128)}, u32[]{:S(2)}) copy-start(s32[1,2]{1,0:T(1,128)} %order_hbm.1) | copy-start | bytes 28
  0.7 7.6 %copy-start.5 = (s32[4]{0:T(128)S(1)}, s32[4]{0:T(128)}, u32[]{:S(2)}) copy-start(s32[4]{0:T(128)} %dil_ref.1) | copy-start | bytes 52
  2.8 8.8 %collective-permute-start = (bf16[64,768]{1,0:T(8,128)(2,1)}, bf16[64,768]{1,0:T(8,128)(2,1)S(1)}, u32[]{:S(2)}, u32[]{:S(2)}) collective-permute-start(bf16[64,768]{1,0:T(8,128)(2,1)} %get-tuple-element.35), channel_id=1, source_target_pairs={{0,15},{1,2},{2,1},{3,4},{4,3},{5,6},{6,5},{7,8},{8,7},{9,10},{10,... | collective-permute-start | bytes 294920 | tf_op jit(solution)/shard_map/ppermute | solution.py:621
  8.3 3.3 %collective-permute-start.1 = (bf16[64,768]{1,0:T(8,128)(2,1)}, bf16[64,768]{1,0:T(8,128)(2,1)S(1)}, u32[]{:S(2)}, u32[]{:S(2)}) collective-permute-start(bf16[64,768]{1,0:T(8,128)(2,1)} %get-tuple-element.36), channel_id=1, source_target_pairs={{0,1},{1,0},{2,3},{3,2},{4,5},{5,4},{6,7},{7,6},{8,9},{9,8},{10,11... | collective-permute-start | bytes 294920 | tf_op jit(solution)/shard_map/ppermute | solution.py:610
  17.3 1.5 %collective-permute-start.2 = (f32[120,256]{1,0:T(8,128)S(1)}, f32[120,256]{1,0:T(8,128)S(1)}, u32[]{:S(2)}, u32[]{:S(2)}) collective-permute-start(f32[120,256]{1,0:T(8,128)S(1)} %get-tuple-element.45), channel_id=1, source_target_pairs={{0,1},{1,0},{2,3},{3,2},{4,5},{5,4},{6,7},{7,6},{8,9},{9,8},{10,11... | collective-permute-start | bytes 368648 | tf_op jit(solution)/shard_map/ppermute | solution.py:610
  18.8 4.2 %collective-permute-start.3 = (f32[104,256]{1,0:T(8,128)S(1)}, f32[104,256]{1,0:T(8,128)S(1)}, u32[]{:S(2)}, u32[]{:S(2)}) collective-permute-start(f32[104,256]{1,0:T(8,128)S(1)} %slice_add_fusion), channel_id=1, source_target_pairs={{0,3},{1,4},{2,7},{3,0},{4,1},{5,6},{6,5},{7,2},{8,13},{9,10},{10,... | collective-permute-start | bytes 319496 | tf_op jit(solution)/shard_map/ppermute | solution.py:615
  23.0 4.5 %collective-permute-start.4 = (f32[104,256]{1,0:T(8,128)S(1)}, f32[104,256]{1,0:T(8,128)S(1)}, u32[]{:S(2)}, u32[]{:S(2)}) collective-permute-start(f32[104,256]{1,0:T(8,128)S(1)} %add.13), channel_id=1, source_target_pairs={{0,5},{1,8},{2,11},{3,6},{4,13},{5,0},{6,3},{7,14},{8,1},{9,12},{1... | collective-permute-start | bytes 319496 | tf_op jit(solution)/shard_map/ppermute | solution.py:615
  23.1 7.2 %collective-permute-start.5 = (bf16[48,256]{1,0:T(8,128)(2,1)S(1)}, bf16[48,256]{1,0:T(8,128)(2,1)S(1)}, u32[]{:S(2)}, u32[]{:S(2)}) collective-permute-start(bf16[48,256]{1,0:T(8,128)(2,1)S(1)} %get-tuple-element.49), channel_id=1, source_target_pairs={{0,15},{1,2},{2,1},{3,4},{4,3},{5,6},{6,5},{7,8},{8,7},{9,10},{10,... | collective-permute-start | bytes 73736 | tf_op jit(solution)/shard_map/ppermute | solution.py:621
  30.3 5.0 %collective-permute-start.6 = (f32[104,256]{1,0:T(8,128)S(1)}, f32[104,256]{1,0:T(8,128)S(1)}, u32[]{:S(2)}, u32[]{:S(2)}) collective-permute-start(f32[104,256]{1,0:T(8,128)S(1)} %add.14), channel_id=1, source_target_pairs={{0,9},{1,2},{2,1},{3,10},{4,7},{5,12},{6,15},{7,4},{8,11},{9,0},{1... | collective-permute-start | bytes 319496 | tf_op jit(solution)/shard_map/ppermute | solution.py:615
  35.4 1.4 %collective-permute-start.7 = (f32[136,256]{1,0:T(8,128)S(1)}, f32[136,256]{1,0:T(8,128)S(1)}, u32[]{:S(2)}, u32[]{:S(2)}) collective-permute-start(f32[136,256]{1,0:T(8,128)S(1)} %pad_maximum_fusion), channel_id=1, source_target_pairs={{0,1},{1,0},{2,3},{3,2},{4,5},{5,4},{6,7},{7,6},{8,9},{9,8},{10,11... | collective-permute-start | bytes 417800 | tf_op jit(solution)/shard_map/ppermute | solution.py:610

commit v4 on v3

--- a/solution.py
+++ b/solution.py
@@ -321,15 +321,13 @@
                     rolled_ref[16 * part + i, to_row : to_row + width, :] = y[
                         width * i : width * (i + 1), LANES * v : LANES * (v + 1)
                     ]
-    part_ref[...] = jnp.zeros_like(part_ref)
-
-    def sum_rows(j, carry):
-        stack = jnp.concatenate([taps_of(rolled_ref, spacing, 2 * j + m) for m in range(2)], 1)
-        grads = jnp.concatenate([dense_ref[2 * j], dense_ref[2 * j + 1]], 1)
-        part_ref[...] += dot(grads, stack, NT)
-        return carry
-
-    lax.fori_loop(0, 8, sum_rows, 0, unroll=4)
+    total = None
+    for j in range(4):
+        rows = range(4 * j, 4 * (j + 1))
+        stack = jnp.concatenate([taps_of(rolled_ref, spacing, r) for r in rows], 1)
+        share = dot(jnp.concatenate([dense_ref[r] for r in rows], 1), stack, NT)
+        total = share if total is None else total + share
+    part_ref[...] = total
 
 
 def taps_of(rolled_ref, spacing, r):

time: 37.8 us -> 37.3 us (0.987)
  Pallas kernels: 15.2 us -> 14.7 us
    pallas_call x6, Pallas kernels: 15.2 us -> 14.7 us  [call(): pl.pallas_call(kernel, out_shape=outs, in_specs=specs, out_specs=[SMEM if...]
where the time goes in v4:
time: 37.3 us; the launch traced here: 37.2 us
  Pallas kernels  14.7 us (39%)
  waiting for transfers between devices  11.7 us (31%)
  starting transfers between devices  9.84 us (26%)
  between operations  0.81 us (2%)
    pallas_call x6, Pallas kernels, call(): pl.pallas_call(kernel, out_shape=outs, in_specs=specs, out_specs=[SMEM if...  14.7 us
    ppermute x2, starting transfers between devices, swap_chips(): return lax.ppermute(shard, 'blk', pairs)  9.08 us
    ppermute x3, waiting for transfers between devices, swap_stage(): return lax.ppermute(shard, 'blk', pairs)  6.91 us
    ppermute x2, waiting for transfers between devices, swap_chips(): return lax.ppermute(shard, 'blk', pairs)  2.82 us
    ppermute x3, waiting for transfers between devices, swap_with(): lax.ppermute(shard, 'blk', [(i, i ^ step) for i in range(lax.axis_size('b...  1.96 us
  transfers between devices with their start and end apart: 8, of which 6 were waited for; matrix products, arithmetic and copies ran while one was open for 0% of the time, Pallas kernels for 18%

profile of v4, /device:TPU:0, one launch (start us, length us, event | category | flops | bytes accessed | tf_op | source)
XLA Modules:
  0.0 37.2 jit_solution(10668192697995277831)
XLA Ops:
  0.6 0.0 copy-start
  0.6 0.0 copy-start.1
  0.7 2.1 %shard_map.94 = (bf16[64,768]{1,0:T(8,128)(2,1)}, bf16[64,768]{1,0:T(8,128)(2,1)}) custom-call(s32[1,2]{1,0:T(1,128)} %order_hbm.1, bf16[2,64,1024]{2,1,0:T(8,128)(2,1)} %bitcast.8, bf16[32,256]{1,0:T(8,128)(2,1)} %own_ref.1), custom_call_target="tpu_custom_call" | custom-call | flops 10000000000 | bytes 1000000 | tf_op jit(solution)/shard_map/pallas_call | solution.py:596
  2.8 5.5 %collective-permute-start = (bf16[64,768]{1,0:T(8,128)(2,1)}, bf16[64,768]{1,0:T(8,128)(2,1)S(1)}, u32[]{:S(2)}, u32[]{:S(2)}) collective-permute-start(bf16[64,768]{1,0:T(8,128)(2,1)} %get-tuple-element.35), channel_id=1, source_target_pairs={{0,15},{1,2},{2,1},{3,4},{4,3},{5,6},{6,5},{7,8},{8,7},{9,10},{10,... | collective-permute-start | bytes 294920 | tf_op jit(solution)/shard_map/ppermute | solution.py:619
  8.3 0.0 collective-permute-start.1
  8.3 3.2 %shard_map.93 = (bf16[32,64,128]{2,1,0:T(8,128)(2,1)S(1)}, bf16[16,64,128]{2,1,0:T(8,128)(2,1)S(1)}, bf16[8,64,128]{2,1,0:T(8,128)(2,1)S(1)}, bf16[64,576]{1,0:T...) custom-call(s32[1,2]{1,0:T(1,128)S(1)} %copy-done.4, ...), custom_call_target="tpu_custom_call" | custom-call | flops 200000000 | bytes 3000000 | tf_op jit(solution)/shard_map/pallas_call | solution.py:596
  11.5 0.0 collective-permute-done.chip_ref
  11.5 0.0 collective-permute-done.1.core_ref
  11.6 5.3 %shard_map.95 = (f32[104,256]{1,0:T(8,128)S(1)}, f32[120,256]{1,0:T(8,128)S(1)}, f32[16,256]{1,0:T(8,128)S(1)}, f32[32,256]{1,0:T(8,128)S(1)}, bf16[2048,128]{1,...) custom-call(s32[8]{0:T(128)S(1)} %get-tuple-element.33.meta_ref, ...), custom_call_target="tpu_custom_call" | custom-call | flops 2000000000 | bytes 8000000 | tf_op jit(solution)/shard_map/pallas_call | solution.py:596
  16.8 0.5 %collective-permute-start.2 = (f32[120,256]{1,0:T(8,128)S(1)}, f32[120,256]{1,0:T(8,128)S(1)}, u32[]{:S(2)}, u32[]{:S(2)}) collective-permute-start(f32[120,256]{1,0:T(8,128)S(1)} %get-tuple-element.45), channel_id=1, source_target_pairs={{0,1},{1,0},{2,3},{3,2},{4,5},{5,4},{6,7},{7,6},{8,9},{9,8},{10,11... | collective-permute-start | bytes 368648 | tf_op jit(solution)/shard_map/ppermute | solution.py:608
  17.4 0.3 shard_map.96
  17.7 0.6 %collective-permute-done.2 = f32[120,256]{1,0:T(8,128)S(1)} collective-permute-done((f32[120,256]{1,0:T(8,128)S(1)}, f32[120,256]{1,0:T(8,128)S(1)}, u32[]{:S(2)}, u32[]{:S(2)}) %collective-permute-start.2) | collective-permute-done | bytes 122912 | tf_op jit(solution)/shard_map/ppermute | solution.py:608
  18.4 0.1 collective-permute-start.3
  18.4 4.1 %collective-permute-done.3 = f32[104,256]{1,0:T(8,128)S(1)} collective-permute-done((f32[104,256]{1,0:T(8,128)S(1)}, f32[104,256]{1,0:T(8,128)S(1)}, u32[]{:S(2)}, u32[]{:S(2)}) %collective-permute-start.3) | collective-permute-done | bytes 106528 | tf_op jit(solution)/shard_map/ppermute | solution.py:613
  22.6 0.1 collective-permute-start.4
  22.6 3.6 %collective-permute-start.5 = (bf16[48,256]{1,0:T(8,128)(2,1)S(1)}, bf16[48,256]{1,0:T(8,128)(2,1)S(1)}, u32[]{:S(2)}, u32[]{:S(2)}) collective-permute-start(bf16[48,256]{1,0:T(8,128)(2,1)S(1)} %get-tuple-element.49), channel_id=1, source_target_pairs={{0,15},{1,2},{2,1},{3,4},{4,3},{5,6},{6,5},{7,8},{8,7},{9,10},{10,... | collective-permute-start | bytes 73736 | tf_op jit(solution)/shard_map/ppermute | solution.py:619
  26.2 0.8 %collective-permute-done.4 = f32[104,256]{1,0:T(8,128)S(1)} collective-permute-done((f32[104,256]{1,0:T(8,128)S(1)}, f32[104,256]{1,0:T(8,128)S(1)}, u32[]{:S(2)}, u32[]{:S(2)}) %collective-permute-start.4) | collective-permute-done | bytes 106528 | tf_op jit(solution)/shard_map/ppermute | solution.py:613
  27.0 2.8 %collective-permute-done.5 = bf16[48,256]{1,0:T(8,128)(2,1)S(1)} collective-permute-done((bf16[48,256]{1,0:T(8,128)(2,1)S(1)}, bf16[48,256]{1,0:T(8,128)(2,1)S(1)}, u32[]{:S(2)}, u32[]{:S(2)}) %collective-permute-start.5) | collective-permute-done | bytes 24608 | tf_op jit(solution)/shard_map/ppermute | solution.py:619
  29.9 0.0 collective-permute-start.6
  29.9 3.0 %shard_map.97 = bf16[2,64,1024]{2,1,0:T(8,128)(2,1)} custom-call(s32[8]{0:T(128)S(1)} %get-tuple-element.33.meta_ref, bf16[64,576]{1,0:T(8,128)(2,1)S(1)} %get-tuple-element.34.flat_ref, bf16[32,192,128]{2,1,0:T(8,128)(2,1)S(1)} %get-tuple-element.51.rolled_ref, bf16[32,64,128]{2,1,0:T(8,128)(2,1)S(1)} %get-tuple-element.52.pair_ref, ...), custom_call_target="tpu_custom_call" | custom-call | flops 200000000 | bytes 2000000 | tf_op jit(solution)/shard_map/pallas_call | solution.py:596
  32.9 2.0 %collective-permute-done.6 = f32[104,256]{1,0:T(8,128)S(1)} collective-permute-done((f32[104,256]{1,0:T(8,128)S(1)}, f32[104,256]{1,0:T(8,128)S(1)}, u32[]{:S(2)}, u32[]{:S(2)}) %collective-permute-start.6) | collective-permute-done | bytes 106528 | tf_op jit(solution)/shard_map/ppermute | solution.py:613
  34.9 0.1 collective-permute-start.7
  35.0 1.3 %collective-permute-done.7.other_ref = f32[136,256]{1,0:T(8,128)S(1)} collective-permute-done((f32[136,256]{1,0:T(8,128)S(1)}, f32[136,256]{1,0:T(8,128)S(1)}, u32[]{:S(2)}, u32[]{:S(2)}) %collective-permute-start.7) | collective-permute-done | bytes 139296 | tf_op jit(solution)/shard_map/ppermute | solution.py:608
  36.3 0.8 %shard_map.98 = (f32[64,256]{1,0:T(8,128)}, f32[9,64,64]{2,1,0:T(8,128)}, f32[32,256]{1,0:T(8,128)}) custom-call(f32[104,256]{1,0:T(8,128)S(1)} %add.15.mine_ref, f32[136,256]{1,0:T(8,128)S(1)} %collective-permute-done.7.other_ref, bf16[32,256]{1,0:T(8,128)(2,1)S(1)} %slice.15.chip_ref, f32[32,256]{1,0:T(8,128)S(1)} %get-tuple-element.58.near_ref), custom_call_target="tpu_custom_call" | custom-call | bytes 1000000 | tf_op jit(solution)/shard_map/pallas_call | solution.py:596
  (18 shorter events, 0.1 us)
Async XLA Ops:
  0.6 7.6 %copy-start = (bf16[256,64]{0,1:T(8,128)(2,1)S(1)}, bf16[256,64]{0,1:T(8,128)(2,1)}, u32[]{:S(2)}) copy-start(bf16[256,64]{0,1:T(8,128)(2,1)} %param.7) | copy-start | bytes 98308
  0.6 7.6 %copy-start.1 = (bf16[32,256]{1,0:T(8,128)(2,1)S(1)}, bf16[32,256]{1,0:T(8,128)(2,1)}, u32[]{:S(2)}) copy-start(bf16[32,256]{1,0:T(8,128)(2,1)} %own_ref.1) | copy-start | bytes 49156
  0.7 7.6 %copy-start.2 = (bf16[1,2,64,1024]{3,2,1,0:T(8,128)(2,1)S(1)}, bf16[1,2,64,1024]{3,2,1,0:T(8,128)(2,1)}, u32[]{:S(2)}) copy-start(bf16[1,2,64,1024]{3,2,1,0:T(8,128)(2,1)} %param.11) | copy-start | bytes 786436
  0.7 7.6 %copy-start.3 = (bf16[64,9,64]{2,0,1:T(8,128)(2,1)S(1)}, bf16[64,9,64]{2,0,1:T(8,128)(2,1)}, u32[]{:S(2)}) copy-start(bf16[64,9,64]{2,0,1:T(8,128)(2,1)} %param.8) | copy-start | bytes 221188
  0.7 7.6 %copy-start.4 = (s32[1,2]{1,0:T(1,128)S(1)}, s32[1,2]{1,0:T(1,128)}, u32[]{:S(2)}) copy-start(s32[1,2]{1,0:T(1,128)} %order_hbm.1) | copy-start | bytes 28
  0.7 7.6 %copy-start.5 = (s32[4]{0:T(128)S(1)}, s32[4]{0:T(128)}, u32[]{:S(2)}) copy-start(s32[4]{0:T(128)} %dil_ref.1) | copy-start | bytes 52
  2.8 8.8 %collective-permute-start = (bf16[64,768]{1,0:T(8,128)(2,1)}, bf16[64,768]{1,0:T(8,128)(2,1)S(1)}, u32[]{:S(2)}, u32[]{:S(2)}) collective-permute-start(bf16[64,768]{1,0:T(8,128)(2,1)} %get-tuple-element.35), channel_id=1, source_target_pairs={{0,15},{1,2},{2,1},{3,4},{4,3},{5,6},{6,5},{7,8},{8,7},{9,10},{10,... | collective-permute-start | bytes 294920 | tf_op jit(solution)/shard_map/ppermute | solution.py:619
  8.3 3.3 %collective-permute-start.1 = (bf16[64,768]{1,0:T(8,128)(2,1)}, bf16[64,768]{1,0:T(8,128)(2,1)S(1)}, u32[]{:S(2)}, u32[]{:S(2)}) collective-permute-start(bf16[64,768]{1,0:T(8,128)(2,1)} %get-tuple-element.36), channel_id=1, source_target_pairs={{0,1},{1,0},{2,3},{3,2},{4,5},{5,4},{6,7},{7,6},{8,9},{9,8},{10,11... | collective-permute-start | bytes 294920 | tf_op jit(solution)/shard_map/ppermute | solution.py:608
  16.8 1.5 %collective-permute-start.2 = (f32[120,256]{1,0:T(8,128)S(1)}, f32[120,256]{1,0:T(8,128)S(1)}, u32[]{:S(2)}, u32[]{:S(2)}) collective-permute-start(f32[120,256]{1,0:T(8,128)S(1)} %get-tuple-element.45), channel_id=1, source_target_pairs={{0,1},{1,0},{2,3},{3,2},{4,5},{5,4},{6,7},{7,6},{8,9},{9,8},{10,11... | collective-permute-start | bytes 368648 | tf_op jit(solution)/shard_map/ppermute | solution.py:608
  18.4 4.2 %collective-permute-start.3 = (f32[104,256]{1,0:T(8,128)S(1)}, f32[104,256]{1,0:T(8,128)S(1)}, u32[]{:S(2)}, u32[]{:S(2)}) collective-permute-start(f32[104,256]{1,0:T(8,128)S(1)} %slice_add_fusion), channel_id=1, source_target_pairs={{0,3},{1,4},{2,7},{3,0},{4,1},{5,6},{6,5},{7,2},{8,13},{9,10},{10,... | collective-permute-start | bytes 319496 | tf_op jit(solution)/shard_map/ppermute | solution.py:613
  22.6 4.5 %collective-permute-start.4 = (f32[104,256]{1,0:T(8,128)S(1)}, f32[104,256]{1,0:T(8,128)S(1)}, u32[]{:S(2)}, u32[]{:S(2)}) collective-permute-start(f32[104,256]{1,0:T(8,128)S(1)} %add.13), channel_id=1, source_target_pairs={{0,5},{1,8},{2,11},{3,6},{4,13},{5,0},{6,3},{7,14},{8,1},{9,12},{1... | collective-permute-start | bytes 319496 | tf_op jit(solution)/shard_map/ppermute | solution.py:613
  22.6 7.2 %collective-permute-start.5 = (bf16[48,256]{1,0:T(8,128)(2,1)S(1)}, bf16[48,256]{1,0:T(8,128)(2,1)S(1)}, u32[]{:S(2)}, u32[]{:S(2)}) collective-permute-start(bf16[48,256]{1,0:T(8,128)(2,1)S(1)} %get-tuple-element.49), channel_id=1, source_target_pairs={{0,15},{1,2},{2,1},{3,4},{4,3},{5,6},{6,5},{7,8},{8,7},{9,10},{10,... | collective-permute-start | bytes 73736 | tf_op jit(solution)/shard_map/ppermute | solution.py:619
  29.9 5.0 %collective-permute-start.6 = (f32[104,256]{1,0:T(8,128)S(1)}, f32[104,256]{1,0:T(8,128)S(1)}, u32[]{:S(2)}, u32[]{:S(2)}) collective-permute-start(f32[104,256]{1,0:T(8,128)S(1)} %add.14), channel_id=1, source_target_pairs={{0,9},{1,2},{2,1},{3,10},{4,7},{5,12},{6,15},{7,4},{8,11},{9,0},{1... | collective-permute-start | bytes 319496 | tf_op jit(solution)/shard_map/ppermute | solution.py:613
  34.9 1.4 %collective-permute-start.7 = (f32[136,256]{1,0:T(8,128)S(1)}, f32[136,256]{1,0:T(8,128)S(1)}, u32[]{:S(2)}, u32[]{:S(2)}) collective-permute-start(f32[136,256]{1,0:T(8,128)S(1)} %pad_maximum_fusion), channel_id=1, source_target_pairs={{0,1},{1,0},{2,3},{3,2},{4,5},{5,4},{6,7},{7,6},{8,9},{9,8},{10,11... | collective-permute-start | bytes 417800 | tf_op jit(solution)/shard_map/ppermute | solution.py:608
